TPU v7x, 256 devices: a whole 4x4x8 slice. The times are simulated.
256 devices in a mesh: rec: 8 (over y, core), tm: 32 (over z, x).
Axes of the slice: x: 4, y: 4, z: 8, core: 2. Of those that a mesh axis runs over, the one named last changes fastest.
Arguments:
- wave: float32 [128, 1048576], P('rec', 'tm'), parts along dimension 0, may hold values from -6 to 6
- target_mod: float32 [12288, 1024], P(('rec', 'tm')), parts along dimension 0, may hold values from 0 to 0.5
- lengths: int32 [128], P('rec'), parts along dimension 0, may hold values from 1024 to 4096, as said below
Outputs:
- grad_wave: float32 [128, 1048576], P('rec', 'tm'), parts along dimension 0
- loss: float32 [128], P('rec'), parts along dimension 0
There are 8 independent parts, one for each index of `rec`. A program takes and returns all parts, laid end to end along the dimension named above; each array names one. Nothing has to cross between parts.
Inputs may be any that keep to these rules, and one draw needn't show every extreme that they name: lengths[r] counts frames from the start of recording r; in every part some recording has all 4096 frames valid.
All inputs are finite; a program needn't handle non-finite values.
Results may differ from a plain program's by a relative error of at most 0.00027.
Values sent between devices are 32-bit elements; how exact they have to be, the bound alone decides.
A program may use at most 128 MiB of HBM per device.

v0:
```python
import math

import jax
import jax.numpy as jnp
from jax import lax
from jax.sharding import PartitionSpec as P

FFT = 512
BANDS = 96


HIGH = lax.Precision.HIGHEST
rate_hz = 16000.0


def from_behind(array, axis, by):
    count = lax.axis_size(axis)
    pairs = [(i, i + by) for i in range(count) if 0 <= i + by < count]
    return lax.ppermute(array, axis, pairs)


def from_everyone(array, axis):
    count = lax.axis_size(axis)
    return lax.all_to_all(
        jnp.broadcast_to(array[None], (count, *array.shape)), axis, 0, 0, tiled=True
    )


def of_everyone(array, axis):
    everything = from_everyone(array, axis)
    return jnp.sum(everything, axis=0)


def in_one(arrays, axis):
    vector, at, finished = (jnp.concatenate([a.reshape(-1) for a in arrays]), 0, [])
    so_far = of_everyone(vector, axis)
    for a in arrays:
        finished.append(so_far[at : at + a.size].reshape(a.shape))
        at += a.size
    return tuple(finished)


def a_weight(freq):
    square = freq * freq
    upper = 12194.0**2 * square * square
    lower = (
        (square + 20.6**2)
        * jnp.sqrt((square + 107.7**2) * (square + 737.9**2))
        * (square + 12194.0**2)
    )
    return upper / lower


def bark_scale(freq):
    return 13.0 * jnp.arctan(0.00076 * freq) + 3.5 * jnp.arctan((freq / 7500.0) ** 2)


def band_table(bins, bands):
    freq = jnp.arange(bins, dtype=jnp.float32) * (rate_hz / (2.0 * bins))
    height = bark_scale(freq)
    top_bark = bark_scale(jnp.asarray(rate_hz / 2.0, jnp.float32))
    centres = (jnp.arange(bands, dtype=jnp.float32) + 0.5) * (top_bark / bands)
    spread = jnp.maximum(0.5, 2.0 * top_bark / bands)
    shape = jnp.maximum(0.0, 1.0 - jnp.abs(height[:, None] - centres[None, :]) / spread)
    weight = 0.1 + a_weight(freq) / a_weight(jnp.asarray(1000.0, jnp.float32))
    return shape * weight[:, None] / jnp.maximum(jnp.sum(shape, axis=0), 1.0)[None, :]


def spectral_table(size):
    bins = size // 2
    index = (
        jnp.arange(size, dtype=jnp.int32)[:, None]
        * jnp.arange(bins, dtype=jnp.int32)[None, :]
        % size
    )
    angle = index.astype(jnp.float32) * (2.0 * math.pi / size)
    return jnp.concatenate([jnp.cos(angle), -jnp.sin(angle)], axis=1) * (1.0 / math.sqrt(size))


def hann_window(size):
    return 0.5 - 0.5 * jnp.cos(jnp.arange(size, dtype=jnp.float32) * (2.0 * math.pi / size))


def modulation_table(times, count, length):
    index = times[:, None] * jnp.arange(1, count + 1, dtype=jnp.int32)[None, :] % length
    angle = index.astype(jnp.float32) * (2.0 * math.pi / length)
    return jnp.concatenate([jnp.cos(angle), -jnp.sin(angle)], axis=1) * (1.0 / math.sqrt(length))


def body(wave, target_mod, lengths):
    records = wave.shape[0]
    half = FFT // 2
    frames_dev = wave.shape[1] // half
    devices = lax.axis_size("tm")
    position = lax.axis_index("tm")
    rows_dev = target_mod.shape[0]
    count = target_mod.shape[1]
    frames_all = frames_dev * devices
    window = hann_window(FFT)
    spectral = spectral_table(FFT)
    filters = band_table(half, BANDS)
    blocks = wave.reshape(records, frames_dev, half)
    following = from_behind(blocks[:, 0, :], "tm", -1)
    extended = jnp.concatenate([blocks, following[:, None, :]], axis=1)
    frames = jnp.concatenate([extended[:, :-1], extended[:, 1:]], axis=2) * window
    spectrum = jnp.einsum("rfn,nk->rfk", frames, spectral, precision=HIGH)
    real_stft = spectrum[..., :half]
    imag_stft = spectrum[..., half:]
    power = real_stft * real_stft + imag_stft * imag_stft
    energy = jnp.einsum("rfk,kb->rbf", power, filters, precision=HIGH)
    envelope = (energy + 0.05) ** 0.3
    times = position * frames_dev + jnp.arange(frames_dev, dtype=jnp.int32)
    valid = (times[None, :] < lengths[:, None]).astype(jnp.float32)
    masked = envelope * valid[:, None, :]
    counts = lengths.astype(jnp.float32) * BANDS
    partial_value = jnp.sum(masked, axis=(1, 2))
    row_ids = position * rows_dev + jnp.arange(rows_dev, dtype=jnp.int32)
    owner = row_ids // BANDS
    picker = (owner[:, None] == jnp.arange(records, dtype=jnp.int32)[None, :]).astype(jnp.float32)
    loudness = of_everyone(partial_value, "tm") / counts + 1e-05
    source = masked / loudness[:, None, None]
    flat = source.reshape(records * BANDS, frames_dev)
    full_table = modulation_table(jnp.arange(frames_all, dtype=jnp.int32), count, frames_all)
    stacked = flat.reshape(devices, rows_dev, frames_dev)
    spectra = jnp.dot(
        lax.all_to_all(stacked, "tm", split_axis=0, concat_axis=2, tiled=True)[0],
        full_table,
        precision=HIGH,
        preferred_element_type=jnp.float32,
    )
    real_mod = spectra[:, :count]
    imag_mod = spectra[:, count:]
    mod_power = real_mod * real_mod + imag_mod * imag_mod
    mismatch = jnp.log1p(mod_power) - target_mod
    factor = 2.0 * mismatch / (1.0 + mod_power)
    grad_real = factor * real_mod
    grad_imag = factor * imag_mod
    loss_part = jnp.dot(0.5 * jnp.sum(mismatch * mismatch, axis=1), picker, precision=HIGH)
    inner_part = jnp.dot(
        jnp.sum(grad_real * real_mod + grad_imag * imag_mod, axis=1), picker, precision=HIGH
    )
    loss, inner = in_one((loss_part, inner_part), "tm")
    grad_spectra = jnp.concatenate([grad_real, grad_imag], axis=1)
    grad_bands = lax.dot_general(
        grad_spectra,
        full_table,
        (((1,), (1,)), ((), ())),
        precision=HIGH,
        preferred_element_type=jnp.float32,
    )
    grad_rows = lax.all_to_all(grad_bands, "tm", split_axis=1, concat_axis=0, tiled=True)
    grad_normed = grad_rows.reshape(records, BANDS, frames_dev)
    grad_env = (
        (grad_normed - (inner / counts)[:, None, None])
        / loudness[:, None, None]
        * valid[:, None, :]
    )
    grad_energy = 0.3 * (energy + 0.05) ** (-0.7) * grad_env
    grad_power = jnp.einsum("rbf,kb->rfk", grad_energy, filters, precision=HIGH)
    grad_spectrum = jnp.concatenate(
        [2.0 * real_stft * grad_power, 2.0 * imag_stft * grad_power], axis=2
    )
    grad_frames = jnp.einsum("rfk,nk->rfn", grad_spectrum, spectral, precision=HIGH) * window
    leading = grad_frames[..., :half]
    trailing = grad_frames[..., half:]
    arrived = from_behind(trailing[:, -1, :], "tm", 1)
    moved = jnp.concatenate([arrived[:, None, :], trailing[:, :-1]], axis=1)
    grad_wave = (leading + moved).reshape(records, frames_dev * half)
    return (grad_wave, loss)


def solution(mesh):
    in_specs = (P("rec", "tm"), P(("rec", "tm"), None), P("rec"))
    out_specs = (P("rec", "tm"), P("rec"))
    return jax.shard_map(body, mesh=mesh, in_specs=in_specs, out_specs=out_specs, check_vma=False)
```

profile of v0, /device:TPU:56, one launch (start us, length us, event | category | flops | bytes accessed | tf_op | source)
XLA Modules:
  0.0 242.0 jit_solution(10759516131886003396)
XLA Ops:
  0.6 0.0 copy-start.1
  0.6 2.2 copy.31
  2.9 4.2 %collective-permute-start = (f32[16,256]{1,0:T(8,128)S(1)}, f32[16,256]{1,0:T(8,128)S(1)}, u32[]{:S(2)}, u32[]{:S(2)}) collective-permute-start(f32[16,256]{1,0:T(8,128)S(1)} %bitcast.67), channel_id=1, source_target_pairs={{1,0},{2,1},{3,2},{4,3},{5,4},{6,5},{7,6},{8,7},{9,8},{10,9},{11,1... | collective-permute-start | bytes 49160 | tf_op jit(solution)/shard_map/ppermute | solution.py:19
  7.1 2.1 sine_negate_fusion.1
  9.3 0.2 fusion.67
  9.5 0.0 copy-done.1
  9.5 0.1 compare_convert_fusion
  9.6 0.0 collective-permute-done
  9.6 9.1 %fusion.13 = f32[16,128,512]{2,1,0:T(8,128)} fusion(f32[16,1,256]{2,1,0:T(1,128)S(1)} %broadcast_in_dim.8, f32[16,128,256]{2,1,0:T(8,128)S(1)} %bitcast.62, f32[512]{0:T(512)S(1)} %multiply_subtract_fusion, f32[512,256]{1,0:T(8,128)S(1)} %get-tuple-element.14, f32[512,256]{1,0:T(8,128)S(1)} %get-tuple-element.15), kind=kOutput, calls=%fused_computation.19 | convolution fusion | flops 6446120960 | bytes 7358464 | tf_op jit(solution)/shard_map/rfn,nk->rfk/dot_general | solution.py:106
  18.7 4.9 %fusion.47 = (f32[16]{0:T(128)S(1)}, f32[96,16,128]{2,0,1:T(8,128)S(1)}) fusion(f32[16,128]{1,0:T(8,128)S(1)} %compare_convert_fusion, f32[16,128,512]{2,1,0:T(8,128)} %fusion.13, f32[96]{0:T(128)S(1)} %broadcast_maximum_fusion, f32[256]{0:T(256)S(1)} %get-tuple-element.17, f32[96]{0:T(128)S(1)} %add_multiply_fusion, f32[256]{0:T(256)S(1)} %get-tuple-element.16), kind=kOutput, calls=%fused_computation.58 | convolution fusion | flops 606314496 | bytes 4991808 | tf_op jit(solution)/shard_map/rfk,kb->rbf/dot_general | solution.py:110
  23.7 0.6 broadcast_in_dim.9
  24.3 11.9 %all-to-all-start = ((f32[32,1,16]{2,1,0:T(1,128)}), f32[32,1,16]{2,1,0:T(1,128)S(1)}, u32[]{:S(2)}, u32[]{:S(2)}) async-start(f32[32,1,16]{2,1,0:T(1,128)} %broadcast_in_dim.9), calls=%async_computation | async-start | bytes 32768 | tf_op jit(solution)/shard_map/all_to_all | solution.py:24
  36.3 8.5 %all-to-all-done = f32[32,1,16]{2,1,0:T(1,128)S(1)} async-done(((f32[32,1,16]{2,1,0:T(1,128)}), f32[32,1,16]{2,1,0:T(1,128)S(1)}, u32[]{:S(2)}, u32[]{:S(2)}) %all-to-all-start) | async-done | bytes 2080 | tf_op jit(solution)/shard_map/all_to_all | solution.py:24
  44.7 0.1 reduce_sum.56
  44.8 1.3 fusion.46
  46.1 5.0 %all-to-all-start.1 = ((f32[32,48,128]{2,1,0:T(8,128)}), f32[32,48,128]{2,1,0:T(8,128)S(1)}, u32[]{:S(2)}, u32[]{:S(2)}) async-start(f32[32,48,128]{2,1,0:T(8,128)} %bitcast.5), calls=%async_computation.1 | async-start | bytes 1572864 | tf_op jit(solution)/shard_map/all_to_all | solution.py:126
  51.1 68.2 %fusion.10 = (f32[4096,1024]{1,0:T(8,128)}, f32[4096,1024]{1,0:T(8,128)}) fusion(s32[1024]{0:T(1024)S(1)} %iota_add_fusion), kind=kLoop, calls=%fused_computation.15 | loop fusion | flops 62914560 | bytes 33558528 | tf_op jit(solution)/shard_map/cos | solution.py:87
  119.3 0.0 all-to-all-done.1
  119.3 0.3 copy.23
  119.5 0.0 copy-start
  119.6 25.0 %fusion.1 = f32[48,2048]{1,0:T(8,128)S(1)} fusion(f32[4096,1024]{1,0:T(8,128)} %get-tuple-element.9, f32[4096,1024]{1,0:T(8,128)} %get-tuple-element.8, f32[6,8,32,128]{3,2,1,0:T(8,128)S(1)} %bitcast.65), kind=kOutput, calls=%fused_computation.2 | convolution fusion | flops 4848615424 | bytes 34734080 | tf_op jit(solution)/shard_map/dot_general | solution.py:125
  144.5 0.0 copy-done
  144.5 0.3 multiply_reduce_fusion
  144.8 0.2 convolution_bitcast_fusion
  145.0 0.2 convolution_bitcast_fusion.1
  145.2 0.1 pad_maximum_fusion.1
  145.3 0.6 broadcast_in_dim.10
  145.9 9.9 %all-to-all-start.3 = ((f32[32,1,32]{2,1,0:T(1,128)}), f32[32,1,32]{2,1,0:T(1,128)S(1)}, u32[]{:S(2)}, u32[]{:S(2)}) async-start(f32[32,1,32]{2,1,0:T(1,128)} %broadcast_in_dim.10), calls=%async_computation.3 | async-start | bytes 32768 | tf_op jit(solution)/shard_map/all_to_all | solution.py:24
  155.8 33.8 %fusion.31 = f32[6,32,8,128]{3,2,1,0:T(8,128)S(1)} fusion(f32[4096,1024]{1,0:T(8,128)} %get-tuple-element.9, f32[4096,1024]{1,0:T(8,128)} %get-tuple-element.8, f32[48,1024]{1,0:T(8,128)S(1)} %get-tuple-element.5, f32[48,1024]{1,0:T(8,128)S(1)} %get-tuple-element.4), kind=kOutput, calls=%fused_computation.37 | convolution fusion | flops 4848713728 | bytes 34734080 | tf_op jit(solution)/shard_map/dot_general | solution.py:144
  189.6 0.9 copy.41
  190.5 0.0 all-to-all-done.3
  190.5 9.8 %all-to-all-start.2 = ((f32[48,32,128]{2,0,1:T(8,128)}), f32[48,32,128]{2,0,1:T(8,128)S(1)}, u32[]{:S(2)}, u32[]{:S(2)}) async-start(f32[48,32,128]{2,0,1:T(8,128)} %bitcast.55), calls=%async_computation.2 | async-start | bytes 1572864 | tf_op jit(solution)/shard_map/all_to_all | solution.py:151
  200.3 0.5 fusion.110
  200.9 18.4 %all-to-all-done.2 = f32[48,32,128]{2,0,1:T(8,128)S(1)} async-done(((f32[48,32,128]{2,0,1:T(8,128)}), f32[48,32,128]{2,0,1:T(8,128)S(1)}, u32[]{:S(2)}, u32[]{:S(2)}) %all-to-all-start.2) | async-done | bytes 786464 | tf_op jit(solution)/shard_map/all_to_all | solution.py:151
  219.3 4.6 %multiply_multiply_fusion.1 = (f32[16,128,256]{2,1,0:T(8,128)S(1)}, f32[16,128,256]{2,1,0:T(8,128)S(1)}) fusion(f32[16,128,512]{2,1,0:T(8,128)} %fusion.13, f32[96]{0:T(128)S(1)} %broadcast_maximum_fusion, f32[256]{0:T(256)S(1)} %get-tuple-element.17, f32[96]{0:T(128)S(1)} %add_multiply_fusion, f32[256]{0:T(256)S(1)} %get-tuple-element.16, ...), kind=kOutput, calls=%fused_computation.33 | convolution fusion | flops 607232000 | bytes 9972608 | tf_op jit(solution)/shard_map/rbf,kb->rfk/dot_general | solution.py:159
  223.9 7.3 %fusion.21 = f32[16,128,512]{2,1,0:T(8,128)S(1)} fusion(f32[16,128,256]{2,1,0:T(8,128)S(1)} %get-tuple-element.7, f32[16,128,256]{2,1,0:T(8,128)S(1)} %get-tuple-element.6, f32[512]{0:T(512)S(1)} %multiply_subtract_fusion, f32[512,256]{1,0:T(8,128)S(1)} %get-tuple-element.14, f32[512,256]{1,0:T(8,128)S(1)} %get-tuple-element.15), kind=kOutput, calls=%fused_computation.26 | convolution fusion | flops 6445072384 | bytes 9439232 | tf_op jit(solution)/shard_map/rfk,nk->rfn/dot_general | solution.py:163
  231.3 2.6 %collective-permute-start.1 = (f32[16,256]{1,0:T(8,128)S(1)}, f32[16,256]{1,0:T(8,128)S(1)}, u32[]{:S(2)}, u32[]{:S(2)}) collective-permute-start(f32[16,256]{1,0:T(8,128)S(1)} %bitcast.68), channel_id=1, source_target_pairs={{0,1},{1,2},{2,3},{3,4},{4,5},{5,6},{6,7},{7,8},{8,9},{9,10},{10,1... | collective-permute-start | bytes 49160 | tf_op jit(solution)/shard_map/ppermute | solution.py:19
  233.8 0.3 slice.54
  234.1 4.9 %collective-permute-done.1 = f32[16,256]{1,0:T(8,128)S(1)} collective-permute-done((f32[16,256]{1,0:T(8,128)S(1)}, f32[16,256]{1,0:T(8,128)S(1)}, u32[]{:S(2)}, u32[]{:S(2)}) %collective-permute-start.1) | collective-permute-done | bytes 16416 | tf_op jit(solution)/shard_map/ppermute | solution.py:19
  239.0 0.4 slice_add_fusion
  239.4 2.5 %copy.33 = f32[2,8,128,256]{3,1,2,0:T(8,128)} copy(f32[2,8,128,256]{3,2,1,0:T(8,128)S(1)} %bitcast.58) | data formatting | bytes 4194304
  (15 shorter events, 0.2 us)
Async XLA Ops:
  0.6 8.8 %copy-start.1 = (s32[16]{0:T(128)S(1)}, s32[16]{0:T(128)}, u32[]{:S(2)}) copy-start(s32[16]{0:T(128)} %param.5) | copy-start | bytes 196
  2.9 6.7 %collective-permute-start = (f32[16,256]{1,0:T(8,128)S(1)}, f32[16,256]{1,0:T(8,128)S(1)}, u32[]{:S(2)}, u32[]{:S(2)}) collective-permute-start(f32[16,256]{1,0:T(8,128)S(1)} %bitcast.67), channel_id=1, source_target_pairs={{1,0},{2,1},{3,2},{4,3},{5,4},{6,5},{7,6},{8,7},{9,8},{10,9},{11,1... | collective-permute-start | bytes 49160 | tf_op jit(solution)/shard_map/ppermute | solution.py:19
  24.3 20.4 %all-to-all-start = ((f32[32,1,16]{2,1,0:T(1,128)}), f32[32,1,16]{2,1,0:T(1,128)S(1)}, u32[]{:S(2)}, u32[]{:S(2)}) async-start(f32[32,1,16]{2,1,0:T(1,128)} %broadcast_in_dim.9), calls=%async_computation | async-start | bytes 32768 | tf_op jit(solution)/shard_map/all_to_all | solution.py:24
  46.1 73.2 %all-to-all-start.1 = ((f32[32,48,128]{2,1,0:T(8,128)}), f32[32,48,128]{2,1,0:T(8,128)S(1)}, u32[]{:S(2)}, u32[]{:S(2)}) async-start(f32[32,48,128]{2,1,0:T(8,128)} %bitcast.5), calls=%async_computation.1 | async-start | bytes 1572864 | tf_op jit(solution)/shard_map/all_to_all | solution.py:126
  119.5 25.0 %copy-start = (f32[48,1024]{1,0:T(8,128)S(1)}, f32[48,1024]{1,0:T(8,128)}, u32[]{:S(2)}) copy-start(f32[48,1024]{1,0:T(8,128)} %param.4) | copy-start | bytes 589828
  145.9 44.6 %all-to-all-start.3 = ((f32[32,1,32]{2,1,0:T(1,128)}), f32[32,1,32]{2,1,0:T(1,128)S(1)}, u32[]{:S(2)}, u32[]{:S(2)}) async-start(f32[32,1,32]{2,1,0:T(1,128)} %broadcast_in_dim.10), calls=%async_computation.3 | async-start | bytes 32768 | tf_op jit(solution)/shard_map/all_to_all | solution.py:24
  190.5 28.7 %all-to-all-start.2 = ((f32[48,32,128]{2,0,1:T(8,128)}), f32[48,32,128]{2,0,1:T(8,128)S(1)}, u32[]{:S(2)}, u32[]{:S(2)}) async-start(f32[48,32,128]{2,0,1:T(8,128)} %bitcast.55), calls=%async_computation.2 | async-start | bytes 1572864 | tf_op jit(solution)/shard_map/all_to_all | solution.py:151
  231.3 7.7 %collective-permute-start.1 = (f32[16,256]{1,0:T(8,128)S(1)}, f32[16,256]{1,0:T(8,128)S(1)}, u32[]{:S(2)}, u32[]{:S(2)}) collective-permute-start(f32[16,256]{1,0:T(8,128)S(1)} %bitcast.68), channel_id=1, source_target_pairs={{0,1},{1,2},{2,3},{3,4},{4,5},{5,6},{6,7},{7,8},{8,9},{9,10},{10,1... | collective-permute-start | bytes 49160 | tf_op jit(solution)/shard_map/ppermute | solution.py:19
where the time goes:
time: 242 us
  matrix products  85.2 us (35%)
  other arithmetic  73.3 us (30%)
  starting transfers between devices  43.4 us (18%)
  waiting for transfers between devices  31.8 us (13%)
  local copies, waits for them, and re-layouts  7.52 us (3%)
    cos x1, other arithmetic, modulation_table(): jnp.cos(angle)  68.2 us
    dot_general x1, matrix products, body(): lax.dot_general(grad_spectra, full_table, (((1,), (1,)), ((), ())), preci...  33.8 us
    dot_general x1, matrix products, body(): jnp.dot(lax.all_to_all(stacked, 'tm', split_axis=0, concat_axis=2, tiled=...  25 us
    all_to_all x2, starting transfers between devices, from_everyone(): lax.all_to_all(jnp.broadcast_to(array[None], (count, *array.shape)), axis...  21.8 us
    all_to_all x1, waiting for transfers between devices, body(): lax.all_to_all(grad_bands, 'tm', split_axis=1, concat_axis=0, tiled=True)  18.4 us
    all_to_all x1, starting transfers between devices, body(): lax.all_to_all(grad_bands, 'tm', split_axis=1, concat_axis=0, tiled=True)  9.79 us
    dot_general x1, matrix products, body(): spectrum = jnp.einsum('rfn,nk->rfk', frames, spectral, precision=HIGH)  9.09 us
    all_to_all x2, waiting for transfers between devices, from_everyone(): lax.all_to_all(jnp.broadcast_to(array[None], (count, *array.shape)), axis...  8.47 us
  transfers between devices with their start and end apart: 6, of which 3 were waited for; matrix products, arithmetic and copies ran while one was open for 44% of the time, Pallas kernels for 0%

commit v1 on v0

v1 whole, which is shorter than its diff:
```python
import functools
import math

import jax
import jax.numpy as jnp
import ml_dtypes
import numpy as np
from jax import lax
from jax.experimental import pallas as pl
from jax.experimental.pallas import tpu as pltpu
from jax.sharding import PartitionSpec as P

FFT = 512
HALF = FFT // 2
BANDS = 96
OWN = BANDS // 2
RECORDS = 16
DEVICES = 32
LOCAL = 128
FRAMES = LOCAL * DEVICES
SIDE = 32
SLOT = OWN + 1
RATE = 16000.0
F32 = jnp.float32
BF16 = jnp.bfloat16
MESH = pl.DeviceIdType.MESH


def a_weight(freq):
    square = freq * freq
    upper = 12194.0**2 * square * square
    lower = (
        (square + 20.6**2)
        * np.sqrt((square + 107.7**2) * (square + 737.9**2))
        * (square + 12194.0**2)
    )
    return upper / lower


def bark_scale(freq):
    return 13.0 * np.arctan(0.00076 * freq) + 3.5 * np.arctan((freq / 7500.0) ** 2)


def band_table():
    freq = np.arange(HALF) * (RATE / FFT)
    top = bark_scale(np.float64(RATE / 2.0))
    centres = (np.arange(BANDS) + 0.5) * (top / BANDS)
    spread = max(0.5, 2.0 * top / BANDS)
    shape = np.maximum(0.0, 1.0 - np.abs(bark_scale(freq)[:, None] - centres[None, :]) / spread)
    weight = 0.1 + a_weight(freq) / a_weight(np.float64(1000.0))
    return shape * weight[:, None] / np.maximum(shape.sum(axis=0), 1.0)[None, :]


def two(table):
    high = table.astype(np.float32).astype(ml_dtypes.bfloat16)
    low = (table - high.astype(np.float64)).astype(np.float32).astype(ml_dtypes.bfloat16)
    return high, low


def against(table, axis):
    high, low = two(table)
    return np.concatenate([high, high, low], axis=axis)


def cycle(index, length):
    angle = (index % length) * (2.0 * math.pi / length)
    return np.cos(angle), np.sin(angle)


@functools.cache
def tables():
    n, m = np.arange(HALF)[:, None], np.arange(HALF // 2)[None, :]
    halves = []
    for odd in (0, 1):
        cos, sin = cycle(n * (2 * m + odd), FFT)
        halves.append(np.concatenate([cos, -sin], axis=1) / math.sqrt(FFT))
    forward = np.concatenate([against(h, 0) for h in halves], axis=1)
    backward = np.concatenate([against(h.T, 0) for h in halves], axis=1)
    bands = band_table()
    bands = np.concatenate([bands[0::2], bands[1::2]], axis=0).T
    tau, a = np.arange(LOCAL)[:, None], np.arange(SIDE)[None, :]
    cos, sin = cycle(tau * a, LOCAL)
    cos, sin = cos / math.sqrt(FRAMES), sin / math.sqrt(FRAMES)
    re = np.concatenate([cos, sin], axis=0)
    im = np.concatenate([-sin, cos], axis=0)
    to_bins = np.concatenate([re, im, re, im, im, re, im, re], axis=1)
    high, low = two(np.concatenate([re.T, im.T], axis=0))
    to_time = np.concatenate([high, high, low, np.zeros_like(low)], axis=0)
    cos, sin = cycle((np.arange(SIDE)[:, None] + 1) * np.arange(LOCAL)[None, :], FRAMES)
    turn = np.concatenate([cos, sin], axis=0).astype(np.float32)
    window = 0.5 - 0.5 * np.cos(np.arange(HALF) * (2.0 * math.pi / FFT))
    window = np.broadcast_to(window.astype(np.float32), (8, HALF))
    return (
        forward,
        against(bands, 1),
        against(bands, 0),
        backward,
        against(to_bins, 0),
        to_time,
        turn,
        np.ascontiguousarray(window),
    )


def three(x, axis=-1):
    high = x.astype(BF16)
    low = (x - high.astype(F32)).astype(BF16)
    return jnp.concatenate([high, low, high], axis=axis)


def times(a, b, dims=(((1,), (0,)), ((), ()))):
    return lax.dot_general(a, b, dims, preferred_element_type=F32)


def turned(z, k, n):
    re, im = z
    k = k % n
    if im is None:
        im = jnp.zeros_like(re)
    if k == 0:
        return re, im
    if 4 * k == n:
        return im, -re
    if 2 * k == n:
        return -re, -im
    if 4 * k == 3 * n:
        return -im, re
    c, s = math.cos(2 * math.pi * k / n), math.sin(2 * math.pi * k / n)
    if 8 * k == n:
        return c * (re + im), c * (im - re)
    return c * re + s * im, c * im - s * re


def real_forward(x):
    n = len(x)
    if n == 1:
        return [(x[0], None)]
    if n == 2:
        return [(x[0] + x[1], None), (x[0] - x[1], None)]
    even, odd = real_forward(x[0::2]), real_forward(x[1::2])
    out = [None] * (n // 2 + 1)
    out[0] = (even[0][0] + odd[0][0], None)
    out[n // 2] = (even[0][0] - odd[0][0], None)
    quarter = n // 4
    out[quarter] = (even[quarter][0], -odd[quarter][0])
    for k in range(1, quarter):
        tr, ti = turned(odd[k], k, n)
        er, ei = even[k]
        out[k] = (er + tr, ei + ti)
        out[n // 2 - k] = (er - tr, ti - ei)
    return out


def real_backward(q, n):
    if n == 1:
        return [q[0][0]]
    if n == 2:
        return [q[0][0] + q[1][0], q[0][0] - q[1][0]]
    half, quarter = n // 2, n // 4
    a, b = [], []
    for j in range(quarter + 1):
        (xr, xi), (yr, yi) = q[j], q[half - j]
        if j == 0:
            a.append((xr + yr, None))
            b.append((xr - yr, None))
        elif j == quarter:
            a.append((xr + xr, None))
            b.append((-(xi + xi), None))
        else:
            a.append((xr + yr, xi - yi))
            dr, di = xr - yr, xi + yi
            b.append(turned((dr, di), n - j, n))
    even, odd = real_backward(a, half), real_backward(b, half)
    out = [None] * n
    out[0::2], out[1::2] = even, odd
    return out


def kernel(
    wave,
    target,
    lengths,
    h_forward,
    h_bands,
    h_bands_t,
    h_backward,
    h_bins,
    h_time,
    h_turn,
    h_window,
    out,
    sums,
    forward,
    bands,
    bands_t,
    backward,
    bins,
    to_time,
    turn,
    window,
    wbuf,
    tbuf,
    ttall,
    tperm,
    stft,
    slope,
    send1,
    recv1,
    mid,
    send2,
    recv2,
    obuf,
    edge,
    wave_sem,
    table_sem,
    target_sem,
    halo_sem,
    s1_sem,
    r1_sem,
    s2_sem,
    r2_sem,
    edge_sem,
    out_sem,
):
    me = lax.axis_index("tm")
    pair = me // 2
    side = me % 2
    partner = me + 1 - 2 * side

    barrier = pltpu.get_barrier_semaphore()

    @pl.loop(1, DEVICES)
    def _(j):
        pl.semaphore_signal(
            barrier,
            inc=1,
            device_id={"tm": (me + j) % DEVICES},
            device_id_type=MESH,
        )

    rows = LOCAL * 16
    loads = [
        pltpu.make_async_copy(wave.at[g], wbuf.at[g, pl.ds(0, rows)], wave_sem.at[g])
        for g in range(2)
    ]
    held = [
        pltpu.make_async_copy(src, dst, table_sem.at[i])
        for i, (src, dst) in enumerate(
            (
                (h_forward, forward),
                (h_bands, bands),
                (h_window, window),
                (h_turn, turn),
                (h_bins, bins),
                (h_time, to_time),
                (h_bands_t, bands_t),
                (h_backward, backward),
            )
        )
    ]
    load_target = pltpu.make_async_copy(target, tbuf, target_sem)
    for copy in held[:3] + loads + held[3:] + [load_target]:
        copy.start()

    pl.semaphore_wait(barrier, DEVICES - 1)
    halo = pltpu.make_async_remote_copy(
        src_ref=wave.at[:, pl.ds(0, 16)],
        dst_ref=wbuf.at[:, pl.ds(rows, 16)],
        send_sem=halo_sem.at[0],
        recv_sem=halo_sem.at[1],
        device_id={"tm": (me + DEVICES - 1) % DEVICES},
        device_id_type=MESH,
    )
    halo.start()
    for copy in held + loads + [load_target]:
        copy.wait()
    halo.wait()
    last = me == DEVICES - 1
    wbuf[:, pl.ds(rows, 16), :] = jnp.where(last, 0.0, wbuf[:, pl.ds(rows, 16), :])

    lane = lax.broadcasted_iota(jnp.int32, (1, LOCAL), 1)

    def hops(r, later):
        start = (r % 8) + later * 16
        return jnp.concatenate(
            [wbuf[r // 8, pl.ds(start + 8 * h, LOCAL, stride=16), :] for h in range(2)], axis=1
        )

    def message1(r, s, d):
        return pltpu.make_async_remote_copy(
            src_ref=send1.at[r, s],
            dst_ref=recv1.at[me],
            send_sem=s1_sem.at[d],
            recv_sem=r1_sem.at[me],
            device_id={"tm": d},
            device_id_type=MESH,
        )

    win = window[0:1, :]

    @pl.loop(0, RECORDS // 2)
    def _(i):
        both = [(pair + 1 + 2 * i + e) % RECORDS for e in range(2)]
        now = jnp.concatenate([hops(r, 0) for r in both], axis=0)
        later = jnp.concatenate([hops(r, 1) for r in both], axis=0)
        added = later + win * (now - later)
        taken = win * (now + later) - later
        even = times(three(added), forward[:, 0:HALF])
        odd = times(three(taken), forward[:, HALF:FFT])
        power = [z[:, 0:LOCAL] * z[:, 0:LOCAL] + z[:, LOCAL:] * z[:, LOCAL:] for z in (even, odd)]
        power = three(jnp.concatenate(power, axis=1))
        energy = times(bands[...], power, (((1,), (1,)), ((), ())))
        for e, r in enumerate(both):
            stft[r, :, 0:HALF] = even[e * LOCAL : (e + 1) * LOCAL]
            stft[r, :, HALF:FFT] = odd[e * LOCAL : (e + 1) * LOCAL]
            lifted = energy[:, e * LOCAL : (e + 1) * LOCAL] + 0.05
            valid = (me * LOCAL + lane < lengths[r]).astype(F32)
            masked = jnp.exp(0.3 * jnp.log(lifted)) * valid
            slope[r] = 0.3 * masked / lifted
            total = jnp.sum(masked, axis=0, keepdims=True)
            for s in range(2):
                send1[r, s, 0:OWN, :] = masked[s * OWN : (s + 1) * OWN]
                send1[r, s, OWN:SLOT, :] = total

        for s in range(2):
            message1(both[0], s, 2 * both[0] + s).start()

        @pl.when(i < RECORDS // 2 - 1)
        def _():
            for s in range(2):
                message1(both[1], s, 2 * both[1] + s).start()

    message1(pair, 1 - side, partner).start()
    pltpu.make_async_copy(send1.at[pair, side], recv1.at[me], r1_sem.at[me]).start()

    for i in range(8):
        ttall[pl.ds(i * 128, 128), 0:OWN] = tbuf[:, i * 128 : (i + 1) * 128].T

    @pl.loop(0, SIDE)
    def _(c):
        one = ttall[pl.ds(c, SIDE, stride=SIDE), :]
        tperm[c] = jnp.concatenate([one] * 4, axis=0).T[0:OWN]

    @pl.loop(0, DEVICES)
    def _(j):
        pltpu.make_async_copy(recv1.at[j], recv1.at[j], r1_sem.at[j]).wait()

    @pl.loop(0, OWN // 8)
    def _(i):
        at = pl.ds(pl.multiple_of(i * 8, 8), 8)
        spectrum = real_forward([recv1[p, at, :] for p in range(DEVICES)])
        for c in range(SIDE):
            j = (c + 1) % SIDE
            re, im = spectrum[min(j, SIDE - j)]
            cos, sin = turn[c : c + 1, :], turn[SIDE + c : SIDE + c + 1, :]
            if im is None:
                mid[c, at, 0:LOCAL] = re * cos
                mid[c, at, LOCAL:] = -re * sin
            else:
                if j > SIDE // 2:
                    im = -im
                mid[c, at, 0:LOCAL] = re * cos + im * sin
                mid[c, at, LOCAL:] = im * cos - re * sin

    count = lengths[pair].astype(F32) * BANDS
    total = jnp.sum(recv1[:, OWN:SLOT, :], axis=0)
    loud = jnp.sum(total, axis=1, keepdims=True) / count + 1e-5
    scale = 1.0 / loud
    chunk = 8
    wide = lax.broadcasted_iota(jnp.int32, (chunk * OWN, LOCAL), 1)
    loss = jnp.zeros((8, LOCAL), F32)
    inner = jnp.zeros((8, LOCAL), F32)
    for i in range(SIDE // chunk):
        part = mid[i * chunk : (i + 1) * chunk].reshape(chunk * OWN, HALF)
        z = times(three(part), bins[...]) * scale
        here, other = z[:, 0:LOCAL], z[:, LOCAL:]
        power = here * here + other * other
        above = 1.0 + power
        wanted = tperm[i * chunk : (i + 1) * chunk].reshape(chunk * OWN, LOCAL)
        mismatch = jnp.log(above) - wanted
        factor = 2.0 * mismatch / above
        loss += jnp.sum((mismatch * mismatch).reshape(-1, 8, LOCAL), axis=0)
        inner += jnp.sum((factor * power).reshape(-1, 8, LOCAL), axis=0)
        grad = here * (factor * scale)
        high = grad.astype(BF16)
        first = jnp.where(wide < 2 * SIDE, high.astype(F32), grad - high.astype(F32))
        back = times(jnp.concatenate([first.astype(BF16), high], axis=1), to_time[...])
        mid[i * chunk : (i + 1) * chunk] = back.reshape(chunk, OWN, HALF)
    loss = 0.125 * jnp.sum(jnp.sum(loss, axis=0, keepdims=True), axis=1, keepdims=True)
    inner = 0.25 * jnp.sum(jnp.sum(inner, axis=0, keepdims=True), axis=1, keepdims=True)
    inner = inner / count * scale
    extra = jnp.where(lane == 0, loss, inner)
    send2[:, OWN:SLOT, :] = jnp.broadcast_to(extra[None], (DEVICES, 1, LOCAL))

    @pl.loop(0, OWN // 8)
    def _(i):
        at = pl.ds(pl.multiple_of(i * 8, 8), 8)

        def bin_of(j):
            c = (j - 1) % SIDE
            re, im = mid[c, at, 0:LOCAL], mid[c, at, LOCAL:]
            cos, sin = turn[c : c + 1, :], turn[SIDE + c : SIDE + c + 1, :]
            return re * cos - im * sin, re * sin + im * cos

        paired = [(bin_of(0)[0], None)]
        for j in range(1, SIDE // 2):
            (xr, xi), (yr, yi) = bin_of(j), bin_of(SIDE - j)
            paired.append((0.5 * (xr + yr), 0.5 * (xi - yi)))
        paired.append((bin_of(SIDE // 2)[0], None))
        for p, g in enumerate(real_backward(paired, SIDE)):
            send2[p, at, :] = g

    def message2(d):
        return pltpu.make_async_remote_copy(
            src_ref=send2.at[d],
            dst_ref=recv2.at[me],
            send_sem=s2_sem.at[d],
            recv_sem=r2_sem.at[me],
            device_id={"tm": d},
            device_id_type=MESH,
        )

    @pl.loop(0, RECORDS - 1)
    def _(i):
        q = (pair + 1 + i) % RECORDS
        for s in range(2):
            message2(2 * q + s).start()

    message2(partner).start()
    pltpu.make_async_copy(send2.at[me], recv2.at[me], r2_sem.at[me]).start()

    row = lax.broadcasted_iota(jnp.int32, (LOCAL, HALF), 0)

    @pl.loop(0, RECORDS // 2)
    def _(i):
        both = [(pair + 2 * RECORDS - 1 - 2 * i - e) % RECORDS for e in range(2)]
        powers = []
        for r in both:
            for s in range(2):
                d = 2 * r + s
                pltpu.make_async_copy(recv2.at[d], recv2.at[d], r2_sem.at[d]).wait()
            extras = recv2[2 * r, OWN:SLOT, :] + recv2[2 * r + 1, OWN:SLOT, :]
            sums[pl.ds(r, 1), :] = extras
            mean = extras[:, 1:2]
            grad = jnp.concatenate(
                [recv2[2 * r, 0:OWN, :], recv2[2 * r + 1, 0:OWN, :]], axis=0
            )
            powers.append(three(slope[r] * (grad - mean), axis=0))
        grad = times(
            jnp.concatenate(powers, axis=1), bands_t[...], (((0,), (0,)), ((), ()))
        )
        grad = grad + grad
        pieces = []
        for h in range(2):
            z = jnp.concatenate([stft[r, :, h * HALF : (h + 1) * HALF] for r in both], axis=0)
            g = grad[:, h * LOCAL : (h + 1) * LOCAL]
            z = z * jnp.concatenate([g, g], axis=1)
            pieces.append(times(three(z), backward[:, h * HALF : (h + 1) * HALF]))
        leading = win * (pieces[0] + pieces[1])
        trailing = (1.0 - win) * (pieces[0] - pieces[1])
        for e, r in enumerate(both):
            lead = leading[e * LOCAL : (e + 1) * LOCAL]
            trail = trailing[e * LOCAL : (e + 1) * LOCAL]
            moved = jnp.where(row == 0, 0.0, pltpu.roll(trail, 1, 0))
            full = lead + moved
            for h in range(2):
                start = (r % 8) + 8 * h
                cut = slice(h * LOCAL, (h + 1) * LOCAL)
                obuf[r // 8, pl.ds(start, LOCAL, stride=16), :] = full[:, cut]
                obuf[r // 8, pl.ds(rows + start, 1), :] = trail[LOCAL - 1 : LOCAL, cut]

    over = pltpu.make_async_remote_copy(
        src_ref=obuf.at[:, pl.ds(rows, 16)],
        dst_ref=edge,
        send_sem=edge_sem.at[0],
        recv_sem=edge_sem.at[1],
        device_id={"tm": (me + 1) % DEVICES},
        device_id_type=MESH,
    )
    over.start()
    body = pltpu.make_async_copy(
        obuf.at[:, pl.ds(16, rows - 16)], out.at[:, pl.ds(16, rows - 16)], out_sem.at[0]
    )
    body.start()

    @pl.loop(1, DEVICES)
    def _(j):
        d = (me + j) % DEVICES
        pltpu.make_async_copy(send1.at[d // 2, d % 2], send1.at[d // 2, d % 2], s1_sem.at[d]).wait()
        pltpu.make_async_copy(send2.at[d], send2.at[d], s2_sem.at[d]).wait()

    over.wait()
    obuf[:, pl.ds(0, 16), :] = obuf[:, pl.ds(0, 16), :] + jnp.where(me == 0, 0.0, edge[...])
    head = pltpu.make_async_copy(
        obuf.at[:, pl.ds(0, 16)], out.at[:, pl.ds(0, 16)], out_sem.at[1]
    )
    head.start()
    body.wait()
    head.wait()


def body(wave, target_mod, lengths):
    rows = LOCAL * 16
    wave = wave.reshape(2, 8, LOCAL * 2, 128).transpose(0, 2, 1, 3).reshape(2, rows, 128)
    held = [jnp.asarray(t) for t in tables()]
    space = pl.BlockSpec(memory_space=pl.ANY)
    scratch = [pltpu.VMEM(t.shape, t.dtype) for t in held]
    scratch += [
        pltpu.VMEM((2, rows + 16, 128), F32),
        pltpu.VMEM((OWN, SIDE * SIDE), F32),
        pltpu.VMEM((SIDE * SIDE, 128), F32),
        pltpu.VMEM((SIDE, OWN, 128), F32),
        pltpu.VMEM((RECORDS, LOCAL, FFT), F32),
        pltpu.VMEM((RECORDS, BANDS, LOCAL), F32),
        pltpu.VMEM((RECORDS, 2, SLOT, LOCAL), F32),
        pltpu.VMEM((DEVICES, SLOT, LOCAL), F32),
        pltpu.VMEM((SIDE, OWN, HALF), F32),
        pltpu.VMEM((DEVICES, SLOT, LOCAL), F32),
        pltpu.VMEM((DEVICES, SLOT, LOCAL), F32),
        pltpu.VMEM((2, rows + 16, 128), F32),
        pltpu.VMEM((2, 16, 128), F32),
        pltpu.SemaphoreType.DMA((2,)),
        pltpu.SemaphoreType.DMA((len(held),)),
        pltpu.SemaphoreType.DMA,
        pltpu.SemaphoreType.DMA((2,)),
        pltpu.SemaphoreType.DMA((DEVICES,)),
        pltpu.SemaphoreType.DMA((DEVICES,)),
        pltpu.SemaphoreType.DMA((DEVICES,)),
        pltpu.SemaphoreType.DMA((DEVICES,)),
        pltpu.SemaphoreType.DMA((2,)),
        pltpu.SemaphoreType.DMA((2,)),
    ]
    grad, sums = pl.pallas_call(
        kernel,
        out_shape=(
            jax.ShapeDtypeStruct((2, rows, 128), F32),
            jax.ShapeDtypeStruct((RECORDS, 128), F32),
        ),
        in_specs=[space, space, pl.BlockSpec(memory_space=pltpu.SMEM)] + [space] * len(held),
        out_specs=(space, pl.BlockSpec(memory_space=pltpu.VMEM)),
        scratch_shapes=scratch,
        compiler_params=pltpu.CompilerParams(
            collective_id=0, has_side_effects=True, vmem_limit_bytes=48 * 1024 * 1024
        ),
    )(wave, target_mod, lengths, *held)
    grad = grad.reshape(2, LOCAL * 2, 8, 128).transpose(0, 2, 1, 3).reshape(RECORDS, LOCAL * HALF)
    return grad, sums[:, 0]


def solution(mesh):
    in_specs = (P("rec", "tm"), P(("rec", "tm"), None), P("rec"))
    out_specs = (P("rec", "tm"), P("rec"))
    return jax.shard_map(body, mesh=mesh, in_specs=in_specs, out_specs=out_specs, check_vma=False)
```

time: 242 us -> 79.9 us (0.33)
  the two profiles are of different devices: /device:TPU:56 before, /device:TPU:96 now
where the time goes in v1:
time: 79.9 us; the launch traced here: 79.5 us
  Pallas kernels  67.8 us (85%)
  local copies, waits for them, and re-layouts  11 us (14%)
    pallas_call x1, Pallas kernels, body(): pl.pallas_call(kernel, out_shape=(jax.ShapeDtypeStruct((2, rows, 128), F3...  67.8 us
    unnamed x21, local copies, waits for them, and re-layouts  10.3 us

profile of v1, /device:TPU:96, one launch (start us, length us, event | category | flops | bytes accessed | tf_op | source)
XLA Modules:
  0.0 79.5 jit_solution(12962788660252694155)
XLA Ops:
  0.6 0.0 copy-start
  0.6 1.1 %copy-done = bf16[768,512]{1,0:T(8,128)(2,1)S(1)} copy-done((bf16[768,512]{1,0:T(8,128)(2,1)S(1)}, bf16[768,512]{1,0:T(8,128)(2,1)}, u32[]{:S(2)}) %copy-start) | copy-done | bytes 786456
  1.8 0.0 copy-start.1
  1.8 1.1 %copy-done.1 = bf16[768,512]{1,0:T(8,128)(2,1)S(1)} copy-done((bf16[768,512]{1,0:T(8,128)(2,1)S(1)}, bf16[768,512]{1,0:T(8,128)(2,1)}, u32[]{:S(2)}) %copy-start.1) | copy-done | bytes 786456
  2.9 0.0 copy-start.2
  2.9 1.0 %copy-done.2 = bf16[768,256]{1,0:T(8,128)(2,1)S(1)} copy-done((bf16[768,256]{1,0:T(8,128)(2,1)S(1)}, bf16[768,256]{1,0:T(8,128)(2,1)}, u32[]{:S(2)}) %copy-start.2) | copy-done | bytes 393240
  3.9 0.0 copy-start.3
  3.9 0.9 %copy-done.3 = f32[48,1024]{1,0:T(8,128)S(1)} copy-done((f32[48,1024]{1,0:T(8,128)S(1)}, f32[48,1024]{1,0:T(8,128)}, u32[]{:S(2)}) %copy-start.3) | copy-done | bytes 196632
  4.8 0.0 copy-start.4
  4.8 0.9 %copy-done.4 = bf16[288,256]{1,0:T(8,128)(2,1)S(1)} copy-done((bf16[288,256]{1,0:T(8,128)(2,1)S(1)}, bf16[288,256]{1,0:T(8,128)(2,1)}, u32[]{:S(2)}) %copy-start.4) | copy-done | bytes 147480
  5.7 0.0 copy-start.5
  5.7 0.9 %copy-done.5 = bf16[96,768]{1,0:T(8,128)(2,1)S(1)} copy-done((bf16[96,768]{1,0:T(8,128)(2,1)S(1)}, bf16[96,768]{1,0:T(8,128)(2,1)}, u32[]{:S(2)}) %copy-start.5) | copy-done | bytes 147480
  6.6 0.0 copy-start.6
  6.6 0.9 %copy-done.6 = bf16[256,256]{1,0:T(8,128)(2,1)S(1)} copy-done((bf16[256,256]{1,0:T(8,128)(2,1)S(1)}, bf16[256,256]{1,0:T(8,128)(2,1)}, u32[]{:S(2)}) %copy-start.6) | copy-done | bytes 131096
  7.5 0.0 copy-start.7
  7.6 0.8 copy-done.7
  8.3 0.0 copy-start.8
  8.3 0.7 copy-done.8
  9.0 0.0 copy-start.9
  9.0 0.7 copy-done.9
  9.7 67.8 %shard_map.122 = (f32[2,2048,128]{2,1,0:T(8,128)S(1)}, f32[16,128]{1,0:T(8,128)S(1)}) custom-call(f32[2,2048,128]{2,1,0:T(8,128)} %bitcast.11, f32[48,1024]{1,0:T(8,128)S(1)} %copy-done.3, s32[16]{0:T(128)S(1)} %copy-done.9, bf16[768,512]{1,0:T(8,128)(2,1)S(1)} %copy-done.1, bf16[96,768]{1,0:T(8,128)(2,1)S(1)} %copy-done.5, bf16[288,256]{1,0:T(8,128)(2,1)S(1)} %copy-done.4, ...), custom_call_target="tpu_custom_call" | custom-call | tf_op jit(solution)/shard_map/pallas_call | solution.py:533
  77.5 0.6 slice_reduce_fusion
  78.1 1.3 %copy.14 = f32[16,32768]{1,0:T(8,128)} copy(f32[16,32768]{1,0:T(8,128)S(1)} %bitcast.10) | data formatting | bytes 4194304
Async XLA Ops:
  0.6 1.1 %copy-start = (bf16[768,512]{1,0:T(8,128)(2,1)S(1)}, bf16[768,512]{1,0:T(8,128)(2,1)}, u32[]{:S(2)}) copy-start(bf16[768,512]{1,0:T(8,128)(2,1)} %constant.19.clone.h_backward) | copy-start | bytes 2359300
  1.8 1.1 %copy-start.1 = (bf16[768,512]{1,0:T(8,128)(2,1)S(1)}, bf16[768,512]{1,0:T(8,128)(2,1)}, u32[]{:S(2)}) copy-start(bf16[768,512]{1,0:T(8,128)(2,1)} %constant.16.clone.h_forward) | copy-start | bytes 2359300
  2.9 1.0 %copy-start.2 = (bf16[768,256]{1,0:T(8,128)(2,1)S(1)}, bf16[768,256]{1,0:T(8,128)(2,1)}, u32[]{:S(2)}) copy-start(bf16[768,256]{1,0:T(8,128)(2,1)} %constant.20.clone.h_bins) | copy-start | bytes 1179652
  3.9 0.9 %copy-start.3 = (f32[48,1024]{1,0:T(8,128)S(1)}, f32[48,1024]{1,0:T(8,128)}, u32[]{:S(2)}) copy-start(f32[48,1024]{1,0:T(8,128)} %target.1) | copy-start | bytes 589828
  4.8 0.9 %copy-start.4 = (bf16[288,256]{1,0:T(8,128)(2,1)S(1)}, bf16[288,256]{1,0:T(8,128)(2,1)}, u32[]{:S(2)}) copy-start(bf16[288,256]{1,0:T(8,128)(2,1)} %constant.18.clone.h_bands_t) | copy-start | bytes 442372
  5.7 0.9 %copy-start.5 = (bf16[96,768]{1,0:T(8,128)(2,1)S(1)}, bf16[96,768]{1,0:T(8,128)(2,1)}, u32[]{:S(2)}) copy-start(bf16[96,768]{1,0:T(8,128)(2,1)} %constant.17.clone.h_bands) | copy-start | bytes 442372
  6.6 0.9 %copy-start.6 = (bf16[256,256]{1,0:T(8,128)(2,1)S(1)}, bf16[256,256]{1,0:T(8,128)(2,1)}, u32[]{:S(2)}) copy-start(bf16[256,256]{1,0:T(8,128)(2,1)} %constant.21.clone.h_time) | copy-start | bytes 393220
  7.5 0.8 copy-start.7
  8.3 0.7 copy-start.8
  9.0 0.7 copy-start.9

commit v2 on v1

--- a/solution.py
+++ b/solution.py
@@ -19,7 +19,8 @@
 LOCAL = 128
 FRAMES = LOCAL * DEVICES
 SIDE = 32
-SLOT = OWN + 1
+PART = OWN // 2
+SLOT = PART + 1
 RATE = 16000.0
 F32 = jnp.float32
 BF16 = jnp.bfloat16
@@ -189,7 +190,7 @@
     h_turn,
     h_window,
     out,
-    sums,
+    losses,
     forward,
     bands,
     bands_t,
@@ -204,11 +205,15 @@
     tperm,
     stft,
     slope,
-    send1,
-    recv1,
+    send1a,
+    send1b,
+    recv1a,
+    recv1b,
     mid,
-    send2,
-    recv2,
+    send2a,
+    send2b,
+    recv2a,
+    recv2b,
     obuf,
     edge,
     wave_sem,
@@ -225,7 +230,6 @@
     me = lax.axis_index("tm")
     pair = me // 2
     side = me % 2
-    partner = me + 1 - 2 * side
 
     barrier = pltpu.get_barrier_semaphore()
 
@@ -286,21 +290,57 @@
             [wbuf[r // 8, pl.ds(start + 8 * h, LOCAL, stride=16), :] for h in range(2)], axis=1
         )
 
-    def message1(r, s, d):
+    send1, recv1 = (send1a, send1b), (recv1a, recv1b)
+    send2, recv2 = (send2a, send2b), (recv2a, recv2b)
+
+    def message1(h, r, s):
+        d = 2 * r + s
         return pltpu.make_async_remote_copy(
-            src_ref=send1.at[r, s],
-            dst_ref=recv1.at[me],
-            send_sem=s1_sem.at[d],
-            recv_sem=r1_sem.at[me],
+            src_ref=send1[h].at[r, s],
+            dst_ref=recv1[h].at[me],
+            send_sem=s1_sem.at[h, d],
+            recv_sem=r1_sem.at[h, me],
             device_id={"tm": d},
             device_id_type=MESH,
         )
 
+    def message2(h, d):
+        return pltpu.make_async_remote_copy(
+            src_ref=send2[h].at[d],
+            dst_ref=recv2[h].at[me],
+            send_sem=s2_sem.at[h, d],
+            recv_sem=r2_sem.at[h, me],
+            device_id={"tm": d},
+            device_id_type=MESH,
+        )
+
+    def apart(i):
+        return (pair + i + RECORDS // 2) % RECORDS, (pair + RECORDS // 2 - 1 - i) % RECORDS
+
+    def all_apart(send):
+        @pl.loop(0, RECORDS // 2)
+        def _(i):
+            both = apart(i)
+            for s in range(2):
+                send(both[0], s)
+
+            @pl.when(i < RECORDS // 2 - 1)
+            def _():
+                for s in range(2):
+                    send(both[1], s)
+
+        send(pair, 1 - side)
+
+    def await_all(ref, sem):
+        @pl.loop(0, DEVICES)
+        def _(j):
+            pltpu.make_async_copy(ref.at[j], ref.at[j], sem.at[j]).wait()
+
     win = window[0:1, :]
 
     @pl.loop(0, RECORDS // 2)
     def _(i):
-        both = [(pair + 1 + 2 * i + e) % RECORDS for e in range(2)]
+        both = apart(i)
         now = jnp.concatenate([hops(r, 0) for r in both], axis=0)
         later = jnp.concatenate([hops(r, 1) for r in both], axis=0)
         added = later + win * (now - later)
@@ -319,19 +359,22 @@
             slope[r] = 0.3 * masked / lifted
             total = jnp.sum(masked, axis=0, keepdims=True)
             for s in range(2):
-                send1[r, s, 0:OWN, :] = masked[s * OWN : (s + 1) * OWN]
-                send1[r, s, OWN:SLOT, :] = total
+                send1a[r, s, 0:PART, :] = masked[s * OWN : s * OWN + PART]
+                send1a[r, s, PART:SLOT, :] = total
+                send1b[r, s] = masked[s * OWN + PART : (s + 1) * OWN]
 
         for s in range(2):
-            message1(both[0], s, 2 * both[0] + s).start()
+            message1(0, both[0], s).start()
 
         @pl.when(i < RECORDS // 2 - 1)
         def _():
             for s in range(2):
-                message1(both[1], s, 2 * both[1] + s).start()
-
-    message1(pair, 1 - side, partner).start()
-    pltpu.make_async_copy(send1.at[pair, side], recv1.at[me], r1_sem.at[me]).start()
+                message1(0, both[1], s).start()
+
+    message1(0, pair, 1 - side).start()
+    for h in range(2):
+        pltpu.make_async_copy(send1[h].at[pair, side], recv1[h].at[me], r1_sem.at[h, me]).start()
+    all_apart(lambda r, s: message1(1, r, s).start())
 
     for i in range(8):
         ttall[pl.ds(i * 128, 128), 0:OWN] = tbuf[:, i * 128 : (i + 1) * 128].T
@@ -339,111 +382,112 @@
     @pl.loop(0, SIDE)
     def _(c):
         one = ttall[pl.ds(c, SIDE, stride=SIDE), :]
-        tperm[c] = jnp.concatenate([one] * 4, axis=0).T[0:OWN]
-
-    @pl.loop(0, DEVICES)
-    def _(j):
-        pltpu.make_async_copy(recv1.at[j], recv1.at[j], r1_sem.at[j]).wait()
-
-    @pl.loop(0, OWN // 8)
-    def _(i):
-        at = pl.ds(pl.multiple_of(i * 8, 8), 8)
-        spectrum = real_forward([recv1[p, at, :] for p in range(DEVICES)])
-        for c in range(SIDE):
-            j = (c + 1) % SIDE
-            re, im = spectrum[min(j, SIDE - j)]
-            cos, sin = turn[c : c + 1, :], turn[SIDE + c : SIDE + c + 1, :]
-            if im is None:
-                mid[c, at, 0:LOCAL] = re * cos
-                mid[c, at, LOCAL:] = -re * sin
-            else:
-                if j > SIDE // 2:
-                    im = -im
-                mid[c, at, 0:LOCAL] = re * cos + im * sin
-                mid[c, at, LOCAL:] = im * cos - re * sin
+        wanted = jnp.concatenate([one] * 4, axis=0).T
+        for h in range(2):
+            tperm[h, c] = wanted[h * PART : (h + 1) * PART]
 
     count = lengths[pair].astype(F32) * BANDS
-    total = jnp.sum(recv1[:, OWN:SLOT, :], axis=0)
+    chunk = 16
+    wide = lax.broadcasted_iota(jnp.int32, (chunk * PART, LOCAL), 1)
+
+    def over_devices(h):
+        @pl.loop(0, PART // 8)
+        def _(i):
+            at = pl.ds(pl.multiple_of(i * 8, 8), 8)
+            spectrum = real_forward([recv1[h][p, at, :] for p in range(DEVICES)])
+            for c in range(SIDE):
+                j = (c + 1) % SIDE
+                re, im = spectrum[min(j, SIDE - j)]
+                cos, sin = turn[c : c + 1, :], turn[SIDE + c : SIDE + c + 1, :]
+                if im is None:
+                    mid[h, c, at, 0:LOCAL] = re * cos
+                    mid[h, c, at, LOCAL:] = -re * sin
+                else:
+                    if j > SIDE // 2:
+                        im = -im
+                    mid[h, c, at, 0:LOCAL] = re * cos + im * sin
+                    mid[h, c, at, LOCAL:] = im * cos - re * sin
+
+    def in_device(h, scale):
+        loss = jnp.zeros((8, LOCAL), F32)
+        inner = jnp.zeros((8, LOCAL), F32)
+        for i in range(SIDE // chunk):
+            part = mid[h, i * chunk : (i + 1) * chunk].reshape(chunk * PART, HALF)
+            z = times(three(part), bins[...]) * scale
+            here, other = z[:, 0:LOCAL], z[:, LOCAL:]
+            power = here * here + other * other
+            above = 1.0 + power
+            wanted = tperm[h, i * chunk : (i + 1) * chunk].reshape(chunk * PART, LOCAL)
+            mismatch = jnp.log(above) - wanted
+            factor = 2.0 * mismatch / above
+            loss += jnp.sum((mismatch * mismatch).reshape(-1, 8, LOCAL), axis=0)
+            inner += jnp.sum((factor * power).reshape(-1, 8, LOCAL), axis=0)
+            grad = here * (factor * scale)
+            high = grad.astype(BF16)
+            first = jnp.where(wide < 2 * SIDE, high.astype(F32), grad - high.astype(F32))
+            back = times(jnp.concatenate([first.astype(BF16), high], axis=1), to_time[...])
+            mid[h, i * chunk : (i + 1) * chunk] = back.reshape(chunk, PART, HALF)
+        return loss, inner
+
+    def to_devices(h):
+        @pl.loop(0, PART // 8)
+        def _(i):
+            at = pl.ds(pl.multiple_of(i * 8, 8), 8)
+
+            def bin_of(j):
+                c = (j - 1) % SIDE
+                re, im = mid[h, c, at, 0:LOCAL], mid[h, c, at, LOCAL:]
+                cos, sin = turn[c : c + 1, :], turn[SIDE + c : SIDE + c + 1, :]
+                return re * cos - im * sin, re * sin + im * cos
+
+            paired = [(bin_of(0)[0], None)]
+            for j in range(1, SIDE // 2):
+                (xr, xi), (yr, yi) = bin_of(j), bin_of(SIDE - j)
+                paired.append((0.5 * (xr + yr), 0.5 * (xi - yi)))
+            paired.append((bin_of(SIDE // 2)[0], None))
+            for p, g in enumerate(real_backward(paired, SIDE)):
+                send2[h][p, at, :] = g
+
+    def back(h):
+        all_apart(lambda r, s: message2(h, 2 * r + s).start())
+        pltpu.make_async_copy(send2[h].at[me], recv2[h].at[me], r2_sem.at[h, me]).start()
+
+    await_all(recv1a, r1_sem.at[0])
+    over_devices(0)
+    total = jnp.sum(recv1a[:, PART:SLOT, :], axis=0)
     loud = jnp.sum(total, axis=1, keepdims=True) / count + 1e-5
     scale = 1.0 / loud
-    chunk = 8
-    wide = lax.broadcasted_iota(jnp.int32, (chunk * OWN, LOCAL), 1)
-    loss = jnp.zeros((8, LOCAL), F32)
-    inner = jnp.zeros((8, LOCAL), F32)
-    for i in range(SIDE // chunk):
-        part = mid[i * chunk : (i + 1) * chunk].reshape(chunk * OWN, HALF)
-        z = times(three(part), bins[...]) * scale
-        here, other = z[:, 0:LOCAL], z[:, LOCAL:]
-        power = here * here + other * other
-        above = 1.0 + power
-        wanted = tperm[i * chunk : (i + 1) * chunk].reshape(chunk * OWN, LOCAL)
-        mismatch = jnp.log(above) - wanted
-        factor = 2.0 * mismatch / above
-        loss += jnp.sum((mismatch * mismatch).reshape(-1, 8, LOCAL), axis=0)
-        inner += jnp.sum((factor * power).reshape(-1, 8, LOCAL), axis=0)
-        grad = here * (factor * scale)
-        high = grad.astype(BF16)
-        first = jnp.where(wide < 2 * SIDE, high.astype(F32), grad - high.astype(F32))
-        back = times(jnp.concatenate([first.astype(BF16), high], axis=1), to_time[...])
-        mid[i * chunk : (i + 1) * chunk] = back.reshape(chunk, OWN, HALF)
+    loss, inner = in_device(0, scale)
+    to_devices(0)
+    back(0)
+    await_all(recv1b, r1_sem.at[1])
+    over_devices(1)
+    more_loss, more_inner = in_device(1, scale)
+    loss, inner = loss + more_loss, inner + more_inner
     loss = 0.125 * jnp.sum(jnp.sum(loss, axis=0, keepdims=True), axis=1, keepdims=True)
     inner = 0.25 * jnp.sum(jnp.sum(inner, axis=0, keepdims=True), axis=1, keepdims=True)
     inner = inner / count * scale
     extra = jnp.where(lane == 0, loss, inner)
-    send2[:, OWN:SLOT, :] = jnp.broadcast_to(extra[None], (DEVICES, 1, LOCAL))
-
-    @pl.loop(0, OWN // 8)
-    def _(i):
-        at = pl.ds(pl.multiple_of(i * 8, 8), 8)
-
-        def bin_of(j):
-            c = (j - 1) % SIDE
-            re, im = mid[c, at, 0:LOCAL], mid[c, at, LOCAL:]
-            cos, sin = turn[c : c + 1, :], turn[SIDE + c : SIDE + c + 1, :]
-            return re * cos - im * sin, re * sin + im * cos
-
-        paired = [(bin_of(0)[0], None)]
-        for j in range(1, SIDE // 2):
-            (xr, xi), (yr, yi) = bin_of(j), bin_of(SIDE - j)
-            paired.append((0.5 * (xr + yr), 0.5 * (xi - yi)))
-        paired.append((bin_of(SIDE // 2)[0], None))
-        for p, g in enumerate(real_backward(paired, SIDE)):
-            send2[p, at, :] = g
-
-    def message2(d):
-        return pltpu.make_async_remote_copy(
-            src_ref=send2.at[d],
-            dst_ref=recv2.at[me],
-            send_sem=s2_sem.at[d],
-            recv_sem=r2_sem.at[me],
-            device_id={"tm": d},
-            device_id_type=MESH,
-        )
-
-    @pl.loop(0, RECORDS - 1)
-    def _(i):
-        q = (pair + 1 + i) % RECORDS
-        for s in range(2):
-            message2(2 * q + s).start()
-
-    message2(partner).start()
-    pltpu.make_async_copy(send2.at[me], recv2.at[me], r2_sem.at[me]).start()
+    send2b[:, PART:SLOT, :] = jnp.broadcast_to(extra[None], (DEVICES, 1, LOCAL))
+    to_devices(1)
+    back(1)
 
     row = lax.broadcasted_iota(jnp.int32, (LOCAL, HALF), 0)
+    losses[...] = jnp.zeros((1, LOCAL), F32)
 
     @pl.loop(0, RECORDS // 2)
     def _(i):
-        both = [(pair + 2 * RECORDS - 1 - 2 * i - e) % RECORDS for e in range(2)]
+        both = [(pair + RECORDS // 2 - i) % RECORDS, (pair + RECORDS // 2 + 1 + i) % RECORDS]
         powers = []
         for r in both:
-            for s in range(2):
-                d = 2 * r + s
-                pltpu.make_async_copy(recv2.at[d], recv2.at[d], r2_sem.at[d]).wait()
-            extras = recv2[2 * r, OWN:SLOT, :] + recv2[2 * r + 1, OWN:SLOT, :]
-            sums[pl.ds(r, 1), :] = extras
+            for d in (2 * r, 2 * r + 1):
+                for h in range(2):
+                    pltpu.make_async_copy(recv2[h].at[d], recv2[h].at[d], r2_sem.at[h, d]).wait()
+            extras = recv2b[2 * r, PART:SLOT, :] + recv2b[2 * r + 1, PART:SLOT, :]
+            losses[...] = jnp.where(lane == r, extras[:, 0:1], losses[...])
             mean = extras[:, 1:2]
             grad = jnp.concatenate(
-                [recv2[2 * r, 0:OWN, :], recv2[2 * r + 1, 0:OWN, :]], axis=0
+                [ref[2 * r + s, 0:PART, :] for s in range(2) for ref in recv2], axis=0
             )
             powers.append(three(slope[r] * (grad - mean), axis=0))
         grad = times(
@@ -486,8 +530,10 @@
     @pl.loop(1, DEVICES)
     def _(j):
         d = (me + j) % DEVICES
-        pltpu.make_async_copy(send1.at[d // 2, d % 2], send1.at[d // 2, d % 2], s1_sem.at[d]).wait()
-        pltpu.make_async_copy(send2.at[d], send2.at[d], s2_sem.at[d]).wait()
+        for h in range(2):
+            one, two = send1[h].at[d // 2, d % 2], send2[h].at[d]
+            pltpu.make_async_copy(one, one, s1_sem.at[h, d]).wait()
+            pltpu.make_async_copy(two, two, s2_sem.at[h, d]).wait()
 
     over.wait()
     obuf[:, pl.ds(0, 16), :] = obuf[:, pl.ds(0, 16), :] + jnp.where(me == 0, 0.0, edge[...])
@@ -497,6 +543,19 @@
     head.start()
     body.wait()
     head.wait()
+
+
+def hand_over(grad, losses, out, loss, sem):
+    step = LOCAL * 16 // 4
+    copies = []
+    for i in range(8):
+        at = (i // 4, pl.ds((i % 4) * step, step))
+        copies.append(pltpu.make_async_copy(grad.at[at], out.at[at], sem.at[i]))
+        copies[-1].start()
+    for r in range(RECORDS):
+        loss[r] = losses[0, r]
+    for copy in copies:
+        copy.wait()
 
 
 def body(wave, target_mod, lengths):
@@ -509,13 +568,17 @@
         pltpu.VMEM((2, rows + 16, 128), F32),
         pltpu.VMEM((OWN, SIDE * SIDE), F32),
         pltpu.VMEM((SIDE * SIDE, 128), F32),
-        pltpu.VMEM((SIDE, OWN, 128), F32),
+        pltpu.VMEM((2, SIDE, PART, 128), F32),
         pltpu.VMEM((RECORDS, LOCAL, FFT), F32),
         pltpu.VMEM((RECORDS, BANDS, LOCAL), F32),
         pltpu.VMEM((RECORDS, 2, SLOT, LOCAL), F32),
+        pltpu.VMEM((RECORDS, 2, PART, LOCAL), F32),
         pltpu.VMEM((DEVICES, SLOT, LOCAL), F32),
-        pltpu.VMEM((SIDE, OWN, HALF), F32),
+        pltpu.VMEM((DEVICES, PART, LOCAL), F32),
+        pltpu.VMEM((2, SIDE, PART, HALF), F32),
+        pltpu.VMEM((DEVICES, PART, LOCAL), F32),
         pltpu.VMEM((DEVICES, SLOT, LOCAL), F32),
+        pltpu.VMEM((DEVICES, PART, LOCAL), F32),
         pltpu.VMEM((DEVICES, SLOT, LOCAL), F32),
         pltpu.VMEM((2, rows + 16, 128), F32),
         pltpu.VMEM((2, 16, 128), F32),
@@ -523,28 +586,39 @@
         pltpu.SemaphoreType.DMA((len(held),)),
         pltpu.SemaphoreType.DMA,
         pltpu.SemaphoreType.DMA((2,)),
-        pltpu.SemaphoreType.DMA((DEVICES,)),
-        pltpu.SemaphoreType.DMA((DEVICES,)),
-        pltpu.SemaphoreType.DMA((DEVICES,)),
-        pltpu.SemaphoreType.DMA((DEVICES,)),
+        pltpu.SemaphoreType.DMA((2, DEVICES)),
+        pltpu.SemaphoreType.DMA((2, DEVICES)),
+        pltpu.SemaphoreType.DMA((2, DEVICES)),
+        pltpu.SemaphoreType.DMA((2, DEVICES)),
         pltpu.SemaphoreType.DMA((2,)),
         pltpu.SemaphoreType.DMA((2,)),
     ]
-    grad, sums = pl.pallas_call(
+    grad, losses = pl.pallas_call(
         kernel,
         out_shape=(
             jax.ShapeDtypeStruct((2, rows, 128), F32),
-            jax.ShapeDtypeStruct((RECORDS, 128), F32),
+            jax.ShapeDtypeStruct((1, LOCAL), F32),
         ),
         in_specs=[space, space, pl.BlockSpec(memory_space=pltpu.SMEM)] + [space] * len(held),
         out_specs=(space, pl.BlockSpec(memory_space=pltpu.VMEM)),
         scratch_shapes=scratch,
         compiler_params=pltpu.CompilerParams(
-            collective_id=0, has_side_effects=True, vmem_limit_bytes=48 * 1024 * 1024
+            collective_id=0, has_side_effects=True, vmem_limit_bytes=62 * 1024 * 1024
         ),
     )(wave, target_mod, lengths, *held)
+    grad, loss = pl.pallas_call(
+        hand_over,
+        out_shape=(
+            jax.ShapeDtypeStruct((2, rows, 128), F32),
+            jax.ShapeDtypeStruct((RECORDS,), F32),
+        ),
+        in_specs=[space, pl.BlockSpec(memory_space=pltpu.SMEM)],
+        out_specs=(space, pl.BlockSpec(memory_space=pltpu.SMEM)),
+        scratch_shapes=[pltpu.SemaphoreType.DMA((8,))],
+        compiler_params=pltpu.CompilerParams(vmem_limit_bytes=62 * 1024 * 1024),
+    )(grad, losses)
     grad = grad.reshape(2, LOCAL * 2, 8, 128).transpose(0, 2, 1, 3).reshape(RECORDS, LOCAL * HALF)
-    return grad, sums[:, 0]
+    return grad, loss
 
 
 def solution(mesh):

time: 79.9 us -> 129 us (1.61)
  the two profiles are of different devices: /device:TPU:96 before, /device:TPU:56 now
where the time goes in v2:
time: 129 us; the launch traced here: 127 us
  Pallas kernels  126 us (98%)
    pallas_call x1, Pallas kernels, body(): pl.pallas_call(hand_over, out_shape=(jax.ShapeDtypeStruct((2, rows, 128),...  65.9 us
    pallas_call x1, Pallas kernels, body(): pl.pallas_call(kernel, out_shape=(jax.ShapeDtypeStruct((2, rows, 128), F3...  60.6 us

profile of v2, /device:TPU:56, one launch (start us, length us, event | category | flops | bytes accessed | tf_op | source)
XLA Modules:
  0.0 127.1 jit_solution(98619598221938865)
XLA Ops:
  0.6 60.6 %shard_map.122 = (f32[2,2048,128]{2,1,0:T(8,128)}, f32[1,128]{1,0:T(1,128)}) custom-call(f32[2,2048,128]{2,1,0:T(8,128)} %bitcast.10, f32[48,1024]{1,0:T(8,128)} %target.1, s32[16]{0:T(128)} %lengths.1, bf16[768,512]{1,0:T(8,128)(2,1)} %constant.16.clone.h_forward, bf16[96,768]{1,0:T(8,128)(2,1)} %constant.17.clone.h_bands, ...), custom_call_target="tpu_custom_call" | custom-call | tf_op jit(solution)/shard_map/pallas_call | solution.py:596
  61.3 65.9 %shard_map.123 = (f32[2,2048,128]{2,1,0:T(8,128)}, f32[16]{0:T(128)}) custom-call(f32[2,2048,128]{2,1,0:T(8,128)} %get-tuple-element.6.grad, f32[1,128]{1,0:T(1,128)} %get-tuple-element.7.losses), custom_call_target="tpu_custom_call" | custom-call | tf_op jit(solution)/shard_map/pallas_call | solution.py:609

commit v3 on v2

--- a/solution.py
+++ b/solution.py
@@ -190,6 +190,7 @@
     h_turn,
     h_window,
     out,
+    edge,
     losses,
     forward,
     bands,
@@ -215,7 +216,6 @@
     recv2a,
     recv2b,
     obuf,
-    edge,
     wave_sem,
     table_sem,
     target_sem,
@@ -474,6 +474,14 @@
 
     row = lax.broadcasted_iota(jnp.int32, (LOCAL, HALF), 0)
     losses[...] = jnp.zeros((1, LOCAL), F32)
+    over = pltpu.make_async_remote_copy(
+        src_ref=obuf.at[:, pl.ds(rows, 16)],
+        dst_ref=edge,
+        send_sem=edge_sem.at[0],
+        recv_sem=edge_sem.at[1],
+        device_id={"tm": (me + 1) % DEVICES},
+        device_id_type=MESH,
+    )
 
     @pl.loop(0, RECORDS // 2)
     def _(i):
@@ -494,6 +502,26 @@
             jnp.concatenate(powers, axis=1), bands_t[...], (((0,), (0,)), ((), ()))
         )
         grad = grad + grad
+
+        pieces = []
+        for h in range(2):
+            z = jnp.concatenate([stft[r, LOCAL - 8 :, h * HALF : (h + 1) * HALF] for r in both], axis=0)
+            g = jnp.concatenate(
+                [grad[(e + 1) * LOCAL - 8 : (e + 1) * LOCAL, h * LOCAL : (h + 1) * LOCAL] for e in range(2)],
+                axis=0,
+            )
+            z = z * jnp.concatenate([g, g], axis=1)
+            pieces.append(times(three(z), backward[:, h * HALF : (h + 1) * HALF]))
+        trailing = jnp.where(last, 0.0, (1.0 - win) * (pieces[0] - pieces[1]))
+        for e, r in enumerate(both):
+            for h in range(2):
+                at = pl.ds(rows + 8 * h + r % 8, 1)
+                obuf[r // 8, at, :] = trailing[8 * e + 7 : 8 * e + 8, h * LOCAL : (h + 1) * LOCAL]
+
+        @pl.when(i == RECORDS // 2 - 1)
+        def _():
+            over.start()
+
         pieces = []
         for h in range(2):
             z = jnp.concatenate([stft[r, :, h * HALF : (h + 1) * HALF] for r in both], axis=0)
@@ -511,19 +539,9 @@
                 start = (r % 8) + 8 * h
                 cut = slice(h * LOCAL, (h + 1) * LOCAL)
                 obuf[r // 8, pl.ds(start, LOCAL, stride=16), :] = full[:, cut]
-                obuf[r // 8, pl.ds(rows + start, 1), :] = trail[LOCAL - 1 : LOCAL, cut]
-
-    over = pltpu.make_async_remote_copy(
-        src_ref=obuf.at[:, pl.ds(rows, 16)],
-        dst_ref=edge,
-        send_sem=edge_sem.at[0],
-        recv_sem=edge_sem.at[1],
-        device_id={"tm": (me + 1) % DEVICES},
-        device_id_type=MESH,
-    )
-    over.start()
+
     body = pltpu.make_async_copy(
-        obuf.at[:, pl.ds(16, rows - 16)], out.at[:, pl.ds(16, rows - 16)], out_sem.at[0]
+        obuf.at[:, pl.ds(0, rows)], out, out_sem
     )
     body.start()
 
@@ -536,25 +554,33 @@
             pltpu.make_async_copy(two, two, s2_sem.at[h, d]).wait()
 
     over.wait()
-    obuf[:, pl.ds(0, 16), :] = obuf[:, pl.ds(0, 16), :] + jnp.where(me == 0, 0.0, edge[...])
-    head = pltpu.make_async_copy(
-        obuf.at[:, pl.ds(0, 16)], out.at[:, pl.ds(0, 16)], out_sem.at[1]
-    )
-    head.start()
     body.wait()
-    head.wait()
-
-
-def hand_over(grad, losses, out, loss, sem):
+
+
+def hand_over(grad, edge, losses, out, loss, held, came, sem):
     step = LOCAL * 16 // 4
-    copies = []
-    for i in range(8):
-        at = (i // 4, pl.ds((i % 4) * step, step))
-        copies.append(pltpu.make_async_copy(grad.at[at], out.at[at], sem.at[i]))
-        copies[-1].start()
+    places = [(i // 4, pl.ds((i % 4) * step, step)) for i in range(8)]
+    loads = [
+        pltpu.make_async_copy(grad.at[at], held.at[at], sem.at[0, i])
+        for i, at in enumerate(places)
+    ]
+    stores = [
+        pltpu.make_async_copy(held.at[at], out.at[at], sem.at[1, i])
+        for i, at in enumerate(places)
+    ]
+    arrive = pltpu.make_async_copy(edge, came, sem.at[2, 0])
+    arrive.start()
+    for copy in loads:
+        copy.start()
     for r in range(RECORDS):
         loss[r] = losses[0, r]
-    for copy in copies:
+    arrive.wait()
+    for i, (load, store) in enumerate(zip(loads, stores)):
+        load.wait()
+        if i % 4 == 0:
+            held[i // 4, 0:16, :] = held[i // 4, 0:16, :] + came[i // 4]
+        store.start()
+    for copy in stores:
         copy.wait()
 
 
@@ -581,7 +607,6 @@
         pltpu.VMEM((DEVICES, PART, LOCAL), F32),
         pltpu.VMEM((DEVICES, SLOT, LOCAL), F32),
         pltpu.VMEM((2, rows + 16, 128), F32),
-        pltpu.VMEM((2, 16, 128), F32),
         pltpu.SemaphoreType.DMA((2,)),
         pltpu.SemaphoreType.DMA((len(held),)),
         pltpu.SemaphoreType.DMA,
@@ -591,16 +616,17 @@
         pltpu.SemaphoreType.DMA((2, DEVICES)),
         pltpu.SemaphoreType.DMA((2, DEVICES)),
         pltpu.SemaphoreType.DMA((2,)),
-        pltpu.SemaphoreType.DMA((2,)),
+        pltpu.SemaphoreType.DMA,
     ]
-    grad, losses = pl.pallas_call(
+    grad, edge, losses = pl.pallas_call(
         kernel,
         out_shape=(
             jax.ShapeDtypeStruct((2, rows, 128), F32),
+            jax.ShapeDtypeStruct((2, 16, 128), F32),
             jax.ShapeDtypeStruct((1, LOCAL), F32),
         ),
         in_specs=[space, space, pl.BlockSpec(memory_space=pltpu.SMEM)] + [space] * len(held),
-        out_specs=(space, pl.BlockSpec(memory_space=pltpu.VMEM)),
+        out_specs=(space, space, pl.BlockSpec(memory_space=pltpu.VMEM)),
         scratch_shapes=scratch,
         compiler_params=pltpu.CompilerParams(
             collective_id=0, has_side_effects=True, vmem_limit_bytes=62 * 1024 * 1024
@@ -612,11 +638,15 @@
             jax.ShapeDtypeStruct((2, rows, 128), F32),
             jax.ShapeDtypeStruct((RECORDS,), F32),
         ),
-        in_specs=[space, pl.BlockSpec(memory_space=pltpu.SMEM)],
+        in_specs=[space, space, pl.BlockSpec(memory_space=pltpu.SMEM)],
         out_specs=(space, pl.BlockSpec(memory_space=pltpu.SMEM)),
-        scratch_shapes=[pltpu.SemaphoreType.DMA((8,))],
+        scratch_shapes=[
+            pltpu.VMEM((2, rows, 128), F32),
+            pltpu.VMEM((2, 16, 128), F32),
+            pltpu.SemaphoreType.DMA((3, 8)),
+        ],
         compiler_params=pltpu.CompilerParams(vmem_limit_bytes=62 * 1024 * 1024),
-    )(grad, losses)
+    )(grad, edge, losses)
     grad = grad.reshape(2, LOCAL * 2, 8, 128).transpose(0, 2, 1, 3).reshape(RECORDS, LOCAL * HALF)
     return grad, loss
 

time: 129 us -> 68.7 us (0.53)
  the two profiles are of different devices: /device:TPU:56 before, /device:TPU:16 now
where the time goes in v3:
time: 68.7 us; the launch traced here: 68.5 us
  Pallas kernels  67.8 us (99%)
    pallas_call x1, Pallas kernels, body(): pl.pallas_call(kernel, out_shape=(jax.ShapeDtypeStruct((2, rows, 128), F3...  64.2 us
    pallas_call x1, Pallas kernels, body(): pl.pallas_call(hand_over, out_shape=(jax.ShapeDtypeStruct((2, rows, 128),...  3.66 us

profile of v3, /device:TPU:16, one launch (start us, length us, event | category | flops | bytes accessed | tf_op | source)
XLA Modules:
  0.0 68.5 jit_solution(16384604166358209802)
XLA Ops:
  0.6 64.2 %shard_map.122 = (f32[2,2048,128]{2,1,0:T(8,128)}, f32[2,16,128]{2,1,0:T(8,128)}, f32[1,128]{1,0:T(1,128)}) custom-call(f32[2,2048,128]{2,1,0:T(8,128)} %bitcast.10, f32[48,1024]{1,0:T(8,128)} %target.1, s32[16]{0:T(128)} %lengths.1, bf16[768,512]{1,0:T(8,128)(2,1)} %constant.16.clone.h_forward, bf16[96,768]{1,0:T(8,128)(2,1)} %constant.17.clone.h_bands, ...), custom_call_target="tpu_custom_call" | custom-call | tf_op jit(solution)/shard_map/pallas_call | solution.py:621
  64.8 3.7 %shard_map.123 = (f32[2,2048,128]{2,1,0:T(8,128)}, f32[16]{0:T(128)}) custom-call(f32[2,2048,128]{2,1,0:T(8,128)} %get-tuple-element.7.grad, f32[2,16,128]{2,1,0:T(8,128)} %get-tuple-element.8.edge, f32[1,128]{1,0:T(1,128)} %get-tuple-element.9.losses), custom_call_target="tpu_custom_call" | custom-call | tf_op jit(solution)/shard_map/pallas_call | solution.py:635

commit v4 on v3

--- a/solution.py
+++ b/solution.py
@@ -483,14 +483,15 @@
         device_id_type=MESH,
     )
 
-    @pl.loop(0, RECORDS // 2)
-    def _(i):
-        both = [(pair + RECORDS // 2 - i) % RECORDS, (pair + RECORDS // 2 + 1 + i) % RECORDS]
-        powers = []
+    def await_back(both):
         for r in both:
             for d in (2 * r, 2 * r + 1):
                 for h in range(2):
                     pltpu.make_async_copy(recv2[h].at[d], recv2[h].at[d], r2_sem.at[h, d]).wait()
+
+    def grad_power(both):
+        powers = []
+        for r in both:
             extras = recv2b[2 * r, PART:SLOT, :] + recv2b[2 * r + 1, PART:SLOT, :]
             losses[...] = jnp.where(lane == r, extras[:, 0:1], losses[...])
             mean = extras[:, 1:2]
@@ -498,47 +499,66 @@
                 [ref[2 * r + s, 0:PART, :] for s in range(2) for ref in recv2], axis=0
             )
             powers.append(three(slope[r] * (grad - mean), axis=0))
-        grad = times(
-            jnp.concatenate(powers, axis=1), bands_t[...], (((0,), (0,)), ((), ()))
-        )
-        grad = grad + grad
-
+        grad = times(jnp.concatenate(powers, axis=1), bands_t[...], (((0,), (0,)), ((), ())))
+        return grad + grad
+
+    def to_frames(both, grad, first):
         pieces = []
         for h in range(2):
-            z = jnp.concatenate([stft[r, LOCAL - 8 :, h * HALF : (h + 1) * HALF] for r in both], axis=0)
-            g = jnp.concatenate(
-                [grad[(e + 1) * LOCAL - 8 : (e + 1) * LOCAL, h * LOCAL : (h + 1) * LOCAL] for e in range(2)],
-                axis=0,
-            )
+            z, g = [], []
+            for e, r in enumerate(both):
+                z.append(stft[r, first:, h * HALF : (h + 1) * HALF])
+                g.append(grad[e * LOCAL + first : (e + 1) * LOCAL, h * LOCAL : (h + 1) * LOCAL])
+            z, g = jnp.concatenate(z, axis=0), jnp.concatenate(g, axis=0)
             z = z * jnp.concatenate([g, g], axis=1)
             pieces.append(times(three(z), backward[:, h * HALF : (h + 1) * HALF]))
-        trailing = jnp.where(last, 0.0, (1.0 - win) * (pieces[0] - pieces[1]))
+        return pieces
+
+    def store_edge(r, trail):
+        trail = jnp.where(last, 0.0, trail)
+        for h in range(2):
+            at = pl.ds(rows + 8 * h + r % 8, 1)
+            obuf[r // 8, at, :] = trail[:, h * LOCAL : (h + 1) * LOCAL]
+
+    def back_to_wave(both, grad, edges):
+        plus, minus = to_frames(both, grad, 0)
+        leading = win * (plus + minus)
+        trailing = (1.0 - win) * (plus - minus)
         for e, r in enumerate(both):
-            for h in range(2):
-                at = pl.ds(rows + 8 * h + r % 8, 1)
-                obuf[r // 8, at, :] = trailing[8 * e + 7 : 8 * e + 8, h * LOCAL : (h + 1) * LOCAL]
-
-        @pl.when(i == RECORDS // 2 - 1)
-        def _():
-            over.start()
-
-        pieces = []
-        for h in range(2):
-            z = jnp.concatenate([stft[r, :, h * HALF : (h + 1) * HALF] for r in both], axis=0)
-            g = grad[:, h * LOCAL : (h + 1) * LOCAL]
-            z = z * jnp.concatenate([g, g], axis=1)
-            pieces.append(times(three(z), backward[:, h * HALF : (h + 1) * HALF]))
-        leading = win * (pieces[0] + pieces[1])
-        trailing = (1.0 - win) * (pieces[0] - pieces[1])
-        for e, r in enumerate(both):
-            lead = leading[e * LOCAL : (e + 1) * LOCAL]
             trail = trailing[e * LOCAL : (e + 1) * LOCAL]
             moved = jnp.where(row == 0, 0.0, pltpu.roll(trail, 1, 0))
-            full = lead + moved
+            full = leading[e * LOCAL : (e + 1) * LOCAL] + moved
             for h in range(2):
-                start = (r % 8) + 8 * h
-                cut = slice(h * LOCAL, (h + 1) * LOCAL)
-                obuf[r // 8, pl.ds(start, LOCAL, stride=16), :] = full[:, cut]
+                at = pl.ds((r % 8) + 8 * h, LOCAL, stride=16)
+                obuf[r // 8, at, :] = full[:, h * LOCAL : (h + 1) * LOCAL]
+            if edges:
+                store_edge(r, trail[LOCAL - 1 :])
+
+    def four(i):
+        return [
+            [(pair + RECORDS // 2 - n) % RECORDS, (pair + RECORDS // 2 + 1 + n) % RECORDS]
+            for n in (2 * i, 2 * i + 1)
+        ]
+
+    @pl.loop(0, RECORDS // 4 - 1)
+    def _(i):
+        for both in four(i):
+            await_back(both)
+        for both in four(i):
+            back_to_wave(both, grad_power(both), True)
+
+    final = four(RECORDS // 4 - 1)
+    for both in final:
+        await_back(both)
+    grads = [grad_power(both) for both in final]
+    for both, grad in zip(final, grads):
+        plus, minus = to_frames(both, grad, LOCAL - 8)
+        trailing = (1.0 - win) * (plus - minus)
+        for e, r in enumerate(both):
+            store_edge(r, trailing[8 * e + 7 : 8 * e + 8])
+    over.start()
+    for both, grad in zip(final, grads):
+        back_to_wave(both, grad, False)
 
     body = pltpu.make_async_copy(
         obuf.at[:, pl.ds(0, rows)], out, out_sem

time: 68.7 us -> 65.4 us (0.952)
  Pallas kernels: 67.8 us -> 64.6 us
    pallas_call x1, Pallas kernels: 64.2 us -> 60.9 us  [body(): pl.pallas_call(kernel, out_shape=(jax.ShapeDtypeStruct((2, rows, 128), F3...]
where the time goes in v4:
time: 65.4 us; the launch traced here: 65.2 us
  Pallas kernels  64.6 us (99%)
    pallas_call x1, Pallas kernels, body(): pl.pallas_call(kernel, out_shape=(jax.ShapeDtypeStruct((2, rows, 128), F3...  60.9 us
    pallas_call x1, Pallas kernels, body(): pl.pallas_call(hand_over, out_shape=(jax.ShapeDtypeStruct((2, rows, 128),...  3.66 us

profile of v4, /device:TPU:16, one launch (start us, length us, event | category | flops | bytes accessed | tf_op | source)
XLA Modules:
  0.0 65.2 jit_solution(4406392593151727178)
XLA Ops:
  0.6 60.9 %shard_map.122 = (f32[2,2048,128]{2,1,0:T(8,128)}, f32[2,16,128]{2,1,0:T(8,128)}, f32[1,128]{1,0:T(1,128)}) custom-call(f32[2,2048,128]{2,1,0:T(8,128)} %bitcast.10, f32[48,1024]{1,0:T(8,128)} %target.1, s32[16]{0:T(128)} %lengths.1, bf16[768,512]{1,0:T(8,128)(2,1)} %constant.16.clone.h_forward, bf16[96,768]{1,0:T(8,128)(2,1)} %constant.17.clone.h_bands, ...), custom_call_target="tpu_custom_call" | custom-call | tf_op jit(solution)/shard_map/pallas_call | solution.py:641
  61.5 3.7 %shard_map.123 = (f32[2,2048,128]{2,1,0:T(8,128)}, f32[16]{0:T(128)}) custom-call(f32[2,2048,128]{2,1,0:T(8,128)} %get-tuple-element.7.grad, f32[2,16,128]{2,1,0:T(8,128)} %get-tuple-element.8.edge, f32[1,128]{1,0:T(1,128)} %get-tuple-element.9.losses), custom_call_target="tpu_custom_call" | custom-call | tf_op jit(solution)/shard_map/pallas_call | solution.py:655

commit v5 on v4

--- a/solution.py
+++ b/solution.py
@@ -190,7 +190,6 @@
     h_turn,
     h_window,
     out,
-    edge,
     losses,
     forward,
     bands,
@@ -215,7 +214,8 @@
     send2b,
     recv2a,
     recv2b,
-    obuf,
+    leave,
+    edge,
     wave_sem,
     table_sem,
     target_sem,
@@ -225,7 +225,6 @@
     s2_sem,
     r2_sem,
     edge_sem,
-    out_sem,
 ):
     me = lax.axis_index("tm")
     pair = me // 2
@@ -475,7 +474,7 @@
     row = lax.broadcasted_iota(jnp.int32, (LOCAL, HALF), 0)
     losses[...] = jnp.zeros((1, LOCAL), F32)
     over = pltpu.make_async_remote_copy(
-        src_ref=obuf.at[:, pl.ds(rows, 16)],
+        src_ref=leave,
         dst_ref=edge,
         send_sem=edge_sem.at[0],
         recv_sem=edge_sem.at[1],
@@ -517,8 +516,7 @@
     def store_edge(r, trail):
         trail = jnp.where(last, 0.0, trail)
         for h in range(2):
-            at = pl.ds(rows + 8 * h + r % 8, 1)
-            obuf[r // 8, at, :] = trail[:, h * LOCAL : (h + 1) * LOCAL]
+            leave[r // 8, pl.ds(8 * h + r % 8, 1), :] = trail[:, h * LOCAL : (h + 1) * LOCAL]
 
     def back_to_wave(both, grad, edges):
         plus, minus = to_frames(both, grad, 0)
@@ -530,7 +528,7 @@
             full = leading[e * LOCAL : (e + 1) * LOCAL] + moved
             for h in range(2):
                 at = pl.ds((r % 8) + 8 * h, LOCAL, stride=16)
-                obuf[r // 8, at, :] = full[:, h * LOCAL : (h + 1) * LOCAL]
+                out[r // 8, at, :] = full[:, h * LOCAL : (h + 1) * LOCAL]
             if edges:
                 store_edge(r, trail[LOCAL - 1 :])
 
@@ -560,11 +558,6 @@
     for both, grad in zip(final, grads):
         back_to_wave(both, grad, False)
 
-    body = pltpu.make_async_copy(
-        obuf.at[:, pl.ds(0, rows)], out, out_sem
-    )
-    body.start()
-
     @pl.loop(1, DEVICES)
     def _(j):
         d = (me + j) % DEVICES
@@ -574,33 +567,24 @@
             pltpu.make_async_copy(two, two, s2_sem.at[h, d]).wait()
 
     over.wait()
-    body.wait()
-
-
-def hand_over(grad, edge, losses, out, loss, held, came, sem):
+    out[:, 0:16, :] = out[:, 0:16, :] + edge[...]
+
+
+def hand_over(grad, losses, out, loss, came, kept, sem):
     step = LOCAL * 16 // 4
-    places = [(i // 4, pl.ds((i % 4) * step, step)) for i in range(8)]
-    loads = [
-        pltpu.make_async_copy(grad.at[at], held.at[at], sem.at[0, i])
-        for i, at in enumerate(places)
-    ]
-    stores = [
-        pltpu.make_async_copy(held.at[at], out.at[at], sem.at[1, i])
-        for i, at in enumerate(places)
-    ]
-    arrive = pltpu.make_async_copy(edge, came, sem.at[2, 0])
+    arrive = pltpu.make_async_copy(losses, came, sem.at[8])
     arrive.start()
-    for copy in loads:
-        copy.start()
+    copies = []
+    for i in range(8):
+        at = (i // 4, pl.ds((i % 4) * step, step))
+        copies.append(pltpu.make_async_copy(grad.at[at], out.at[at], sem.at[i]))
+        copies[-1].start()
+    arrive.wait()
     for r in range(RECORDS):
-        loss[r] = losses[0, r]
-    arrive.wait()
-    for i, (load, store) in enumerate(zip(loads, stores)):
-        load.wait()
-        if i % 4 == 0:
-            held[i // 4, 0:16, :] = held[i // 4, 0:16, :] + came[i // 4]
-        store.start()
-    for copy in stores:
+        kept[r] = came[0, r]
+    copies.append(pltpu.make_async_copy(kept, loss, sem.at[9]))
+    copies[-1].start()
+    for copy in copies:
         copy.wait()
 
 
@@ -609,6 +593,7 @@
     wave = wave.reshape(2, 8, LOCAL * 2, 128).transpose(0, 2, 1, 3).reshape(2, rows, 128)
     held = [jnp.asarray(t) for t in tables()]
     space = pl.BlockSpec(memory_space=pl.ANY)
+    in_hbm = functools.partial(pltpu.with_memory_space_constraint, memory_space=pltpu.HBM)
     scratch = [pltpu.VMEM(t.shape, t.dtype) for t in held]
     scratch += [
         pltpu.VMEM((2, rows + 16, 128), F32),
@@ -626,7 +611,8 @@
         pltpu.VMEM((DEVICES, SLOT, LOCAL), F32),
         pltpu.VMEM((DEVICES, PART, LOCAL), F32),
         pltpu.VMEM((DEVICES, SLOT, LOCAL), F32),
-        pltpu.VMEM((2, rows + 16, 128), F32),
+        pltpu.VMEM((2, 16, 128), F32),
+        pltpu.VMEM((2, 16, 128), F32),
         pltpu.SemaphoreType.DMA((2,)),
         pltpu.SemaphoreType.DMA((len(held),)),
         pltpu.SemaphoreType.DMA,
@@ -636,37 +622,34 @@
         pltpu.SemaphoreType.DMA((2, DEVICES)),
         pltpu.SemaphoreType.DMA((2, DEVICES)),
         pltpu.SemaphoreType.DMA((2,)),
-        pltpu.SemaphoreType.DMA,
     ]
-    grad, edge, losses = pl.pallas_call(
+    grad, losses = pl.pallas_call(
         kernel,
         out_shape=(
-            jax.ShapeDtypeStruct((2, rows, 128), F32),
-            jax.ShapeDtypeStruct((2, 16, 128), F32),
+            pltpu.VMEM((2, rows, 128), F32),
             jax.ShapeDtypeStruct((1, LOCAL), F32),
         ),
         in_specs=[space, space, pl.BlockSpec(memory_space=pltpu.SMEM)] + [space] * len(held),
-        out_specs=(space, space, pl.BlockSpec(memory_space=pltpu.VMEM)),
+        out_specs=(pl.BlockSpec(memory_space=pltpu.VMEM),) * 2,
         scratch_shapes=scratch,
         compiler_params=pltpu.CompilerParams(
-            collective_id=0, has_side_effects=True, vmem_limit_bytes=62 * 1024 * 1024
+            collective_id=0, has_side_effects=True, vmem_limit_bytes=54000 * 1024
         ),
-    )(wave, target_mod, lengths, *held)
+    )(in_hbm(wave), in_hbm(target_mod), lengths, *(in_hbm(t) for t in held))
     grad, loss = pl.pallas_call(
         hand_over,
         out_shape=(
             jax.ShapeDtypeStruct((2, rows, 128), F32),
             jax.ShapeDtypeStruct((RECORDS,), F32),
         ),
-        in_specs=[space, space, pl.BlockSpec(memory_space=pltpu.SMEM)],
-        out_specs=(space, pl.BlockSpec(memory_space=pltpu.SMEM)),
+        in_specs=[pl.BlockSpec(memory_space=pltpu.VMEM), space],
+        out_specs=(space, space),
         scratch_shapes=[
-            pltpu.VMEM((2, rows, 128), F32),
-            pltpu.VMEM((2, 16, 128), F32),
-            pltpu.SemaphoreType.DMA((3, 8)),
+            pltpu.SMEM((1, LOCAL), F32),
+            pltpu.SMEM((RECORDS,), F32),
+            pltpu.SemaphoreType.DMA((10,)),
         ],
-        compiler_params=pltpu.CompilerParams(vmem_limit_bytes=62 * 1024 * 1024),
-    )(grad, edge, losses)
+    )(pltpu.with_memory_space_constraint(grad, pltpu.VMEM), losses)
     grad = grad.reshape(2, LOCAL * 2, 8, 128).transpose(0, 2, 1, 3).reshape(RECORDS, LOCAL * HALF)
     return grad, loss
 

time: 65.4 us -> 63 us (0.963)
  the two profiles are of different devices: /device:TPU:16 before, /device:TPU:8 now
where the time goes in v5:
time: 63 us; the launch traced here: 62.9 us
  Pallas kernels  62.3 us (99%)
  between operations  0.64 us (1%)
    pallas_call x1, Pallas kernels, body(): pl.pallas_call(kernel, out_shape=(pltpu.VMEM((2, rows, 128), F32), jax.Sh...  60.8 us
    pallas_call x1, Pallas kernels, body(): pl.pallas_call(hand_over, out_shape=(jax.ShapeDtypeStruct((2, rows, 128),...  1.4 us

profile of v5, /device:TPU:8, one launch (start us, length us, event | category | flops | bytes accessed | tf_op | source)
XLA Modules:
  0.0 62.9 jit_solution(15208771875944098135)
XLA Ops:
  0.6 60.8 %shard_map.122 = (f32[2,2048,128]{2,1,0:T(8,128)S(1)}, f32[1,128]{1,0:T(1,128)}) custom-call(f32[2,2048,128]{2,1,0:T(8,128)} %bitcast.10, f32[48,1024]{1,0:T(8,128)} %target.1, s32[16]{0:T(128)} %lengths.1, bf16[768,512]{1,0:T(8,128)(2,1)} %constant.16.clone.h_forward, bf16[96,768]{1,0:T(8,128)(2,1)} %constant.17.clone.h_bands, ...), custom_call_target="tpu_custom_call" | custom-call | tf_op jit(solution)/shard_map/pallas_call | solution.py:626
  61.5 1.4 %shard_map.123 = (f32[2,2048,128]{2,1,0:T(8,128)}, f32[16]{0:T(128)}) custom-call(f32[2,2048,128]{2,1,0:T(8,128)S(1)} %get-tuple-element.6.grad, f32[1,128]{1,0:T(1,128)} %get-tuple-element.7.losses), custom_call_target="tpu_custom_call" | custom-call | tf_op jit(solution)/shard_map/pallas_call | solution.py:639

commit v6 on v5

--- a/solution.py
+++ b/solution.py
@@ -232,8 +232,7 @@
 
     barrier = pltpu.get_barrier_semaphore()
 
-    @pl.loop(1, DEVICES)
-    def _(j):
+    for j in range(1, DEVICES):
         pl.semaphore_signal(
             barrier,
             inc=1,
@@ -297,8 +296,8 @@
         return pltpu.make_async_remote_copy(
             src_ref=send1[h].at[r, s],
             dst_ref=recv1[h].at[me],
-            send_sem=s1_sem.at[h, d],
-            recv_sem=r1_sem.at[h, me],
+            send_sem=s1_sem.at[h],
+            recv_sem=r1_sem.at[h],
             device_id={"tm": d},
             device_id_type=MESH,
         )
@@ -307,7 +306,7 @@
         return pltpu.make_async_remote_copy(
             src_ref=send2[h].at[d],
             dst_ref=recv2[h].at[me],
-            send_sem=s2_sem.at[h, d],
+            send_sem=s2_sem.at[h],
             recv_sem=r2_sem.at[h, me],
             device_id={"tm": d},
             device_id_type=MESH,
@@ -331,9 +330,7 @@
         send(pair, 1 - side)
 
     def await_all(ref, sem):
-        @pl.loop(0, DEVICES)
-        def _(j):
-            pltpu.make_async_copy(ref.at[j], ref.at[j], sem.at[j]).wait()
+        pltpu.make_async_copy(ref, ref, sem).wait()
 
     win = window[0:1, :]
 
@@ -372,7 +369,7 @@
 
     message1(0, pair, 1 - side).start()
     for h in range(2):
-        pltpu.make_async_copy(send1[h].at[pair, side], recv1[h].at[me], r1_sem.at[h, me]).start()
+        pltpu.make_async_copy(send1[h].at[pair, side], recv1[h].at[me], r1_sem.at[h]).start()
     all_apart(lambda r, s: message1(1, r, s).start())
 
     for i in range(8):
@@ -558,14 +555,10 @@
     for both, grad in zip(final, grads):
         back_to_wave(both, grad, False)
 
-    @pl.loop(1, DEVICES)
-    def _(j):
-        d = (me + j) % DEVICES
-        for h in range(2):
-            one, two = send1[h].at[d // 2, d % 2], send2[h].at[d]
-            pltpu.make_async_copy(one, one, s1_sem.at[h, d]).wait()
-            pltpu.make_async_copy(two, two, s2_sem.at[h, d]).wait()
-
+    others = pl.ds(0, DEVICES - 1)
+    for h in range(2):
+        await_all(recv1[h].at[others], s1_sem.at[h])
+        await_all(recv2[h].at[others], s2_sem.at[h])
     over.wait()
     out[:, 0:16, :] = out[:, 0:16, :] + edge[...]
 
@@ -617,9 +610,9 @@
         pltpu.SemaphoreType.DMA((len(held),)),
         pltpu.SemaphoreType.DMA,
         pltpu.SemaphoreType.DMA((2,)),
-        pltpu.SemaphoreType.DMA((2, DEVICES)),
-        pltpu.SemaphoreType.DMA((2, DEVICES)),
-        pltpu.SemaphoreType.DMA((2, DEVICES)),
+        pltpu.SemaphoreType.DMA((2,)),
+        pltpu.SemaphoreType.DMA((2,)),
+        pltpu.SemaphoreType.DMA((2,)),
         pltpu.SemaphoreType.DMA((2, DEVICES)),
         pltpu.SemaphoreType.DMA((2,)),
     ]

time: 63 us -> 61.3 us (0.973)
  the two profiles are of different devices: /device:TPU:8 before, /device:TPU:16 now
where the time goes in v6:
time: 61.3 us; the launch traced here: 61.2 us
  Pallas kernels  60.6 us (99%)
  between operations  0.64 us (1%)
    pallas_call x1, Pallas kernels, body(): pl.pallas_call(kernel, out_shape=(pltpu.VMEM((2, rows, 128), F32), jax.Sh...  59.2 us
    pallas_call x1, Pallas kernels, body(): pl.pallas_call(hand_over, out_shape=(jax.ShapeDtypeStruct((2, rows, 128),...  1.4 us

profile of v6, /device:TPU:16, one launch (start us, length us, event | category | flops | bytes accessed | tf_op | source)
XLA Modules:
  0.0 61.2 jit_solution(11749315479589411034)
XLA Ops:
  0.6 59.2 %shard_map.122 = (f32[2,2048,128]{2,1,0:T(8,128)S(1)}, f32[1,128]{1,0:T(1,128)}) custom-call(f32[2,2048,128]{2,1,0:T(8,128)} %bitcast.10, f32[48,1024]{1,0:T(8,128)} %target.1, s32[16]{0:T(128)} %lengths.1, bf16[768,512]{1,0:T(8,128)(2,1)} %constant.16.clone.h_forward, bf16[96,768]{1,0:T(8,128)(2,1)} %constant.17.clone.h_bands, ...), custom_call_target="tpu_custom_call" | custom-call | tf_op jit(solution)/shard_map/pallas_call | solution.py:619
  59.8 1.4 %shard_map.123 = (f32[2,2048,128]{2,1,0:T(8,128)}, f32[16]{0:T(128)}) custom-call(f32[2,2048,128]{2,1,0:T(8,128)S(1)} %get-tuple-element.6.grad, f32[1,128]{1,0:T(1,128)} %get-tuple-element.7.losses), custom_call_target="tpu_custom_call" | custom-call | tf_op jit(solution)/shard_map/pallas_call | solution.py:632

commit v7 on v6

--- a/solution.py
+++ b/solution.py
@@ -273,12 +273,27 @@
         device_id={"tm": (me + DEVICES - 1) % DEVICES},
         device_id_type=MESH,
     )
-    halo.start()
+
+    @pl.when(me > 0)
+    def _():
+        halo.start()
+
     for copy in held + loads + [load_target]:
         copy.wait()
-    halo.wait()
-    last = me == DEVICES - 1
-    wbuf[:, pl.ds(rows, 16), :] = jnp.where(last, 0.0, wbuf[:, pl.ds(rows, 16), :])
+
+    @pl.when(me > 0)
+    def _():
+        halo.wait_send()
+
+    @pl.when(me < DEVICES - 1)
+    def _():
+        halo.wait_recv()
+
+
+    @pl.when(me == DEVICES - 1)
+    def _():
+        wbuf[:, pl.ds(rows, 16), :] = jnp.zeros((2, 16, 128), F32)
+
 
     lane = lax.broadcasted_iota(jnp.int32, (1, LOCAL), 1)
 
@@ -511,7 +526,6 @@
         return pieces
 
     def store_edge(r, trail):
-        trail = jnp.where(last, 0.0, trail)
         for h in range(2):
             leave[r // 8, pl.ds(8 * h + r % 8, 1), :] = trail[:, h * LOCAL : (h + 1) * LOCAL]
 
@@ -529,20 +543,21 @@
             if edges:
                 store_edge(r, trail[LOCAL - 1 :])
 
-    def four(i):
+    def group(first, count):
         return [
             [(pair + RECORDS // 2 - n) % RECORDS, (pair + RECORDS // 2 + 1 + n) % RECORDS]
-            for n in (2 * i, 2 * i + 1)
+            for n in (first + m for m in range(count))
         ]
 
-    @pl.loop(0, RECORDS // 4 - 1)
+    @pl.loop(0, 2)
     def _(i):
-        for both in four(i):
+        now = group(2 * i, 2)
+        for both in now:
             await_back(both)
-        for both in four(i):
+        for both in now:
             back_to_wave(both, grad_power(both), True)
 
-    final = four(RECORDS // 4 - 1)
+    final = group(4, 4)
     for both in final:
         await_back(both)
     grads = [grad_power(both) for both in final]
@@ -551,7 +566,11 @@
         trailing = (1.0 - win) * (plus - minus)
         for e, r in enumerate(both):
             store_edge(r, trailing[8 * e + 7 : 8 * e + 8])
-    over.start()
+
+    @pl.when(me < DEVICES - 1)
+    def _():
+        over.start()
+
     for both, grad in zip(final, grads):
         back_to_wave(both, grad, False)
 
@@ -559,8 +578,15 @@
     for h in range(2):
         await_all(recv1[h].at[others], s1_sem.at[h])
         await_all(recv2[h].at[others], s2_sem.at[h])
-    over.wait()
-    out[:, 0:16, :] = out[:, 0:16, :] + edge[...]
+
+    @pl.when(me < DEVICES - 1)
+    def _():
+        over.wait_send()
+
+    @pl.when(me > 0)
+    def _():
+        over.wait_recv()
+        out[:, 0:16, :] = out[:, 0:16, :] + edge[...]
 
 
 def hand_over(grad, losses, out, loss, came, kept, sem):

time: 61.3 us -> 58.5 us (0.954)
  the two profiles are of different devices: /device:TPU:16 before, /device:TPU:56 now
where the time goes in v7:
time: 58.5 us; the launch traced here: 58.4 us
  Pallas kernels  57.8 us (99%)
  between operations  0.64 us (1%)
    pallas_call x1, Pallas kernels, body(): pl.pallas_call(kernel, out_shape=(pltpu.VMEM((2, rows, 128), F32), jax.Sh...  56.4 us
    pallas_call x1, Pallas kernels, body(): pl.pallas_call(hand_over, out_shape=(jax.ShapeDtypeStruct((2, rows, 128),...  1.4 us

profile of v7, /device:TPU:56, one launch (start us, length us, event | category | flops | bytes accessed | tf_op | source)
XLA Modules:
  0.0 58.4 jit_solution(10152678534176119569)
XLA Ops:
  0.6 56.4 %shard_map.122 = (f32[2,2048,128]{2,1,0:T(8,128)S(1)}, f32[1,128]{1,0:T(1,128)}) custom-call(f32[2,2048,128]{2,1,0:T(8,128)} %bitcast.10, f32[48,1024]{1,0:T(8,128)} %target.1, s32[16]{0:T(128)} %lengths.1, bf16[768,512]{1,0:T(8,128)(2,1)} %constant.16.clone.h_forward, bf16[96,768]{1,0:T(8,128)(2,1)} %constant.17.clone.h_bands, ...), custom_call_target="tpu_custom_call" | custom-call | tf_op jit(solution)/shard_map/pallas_call | solution.py:645
  57.0 1.4 %shard_map.123 = (f32[2,2048,128]{2,1,0:T(8,128)}, f32[16]{0:T(128)}) custom-call(f32[2,2048,128]{2,1,0:T(8,128)S(1)} %get-tuple-element.6.grad, f32[1,128]{1,0:T(1,128)} %get-tuple-element.7.losses), custom_call_target="tpu_custom_call" | custom-call | tf_op jit(solution)/shard_map/pallas_call | solution.py:658

commit v8 on v7

--- a/solution.py
+++ b/solution.py
@@ -261,7 +261,7 @@
         )
     ]
     load_target = pltpu.make_async_copy(target, tbuf, target_sem)
-    for copy in held[:3] + loads + held[3:] + [load_target]:
+    for copy in held[:3] + loads:
         copy.start()
 
     pl.semaphore_wait(barrier, DEVICES - 1)
@@ -278,7 +278,9 @@
     def _():
         halo.start()
 
-    for copy in held + loads + [load_target]:
+    for copy in held[3:] + [load_target]:
+        copy.start()
+    for copy in held[:3] + loads:
         copy.wait()
 
     @pl.when(me > 0)
@@ -317,12 +319,12 @@
             device_id_type=MESH,
         )
 
-    def message2(h, d):
+    def message2(h, i, d):
         return pltpu.make_async_remote_copy(
             src_ref=send2[h].at[d],
             dst_ref=recv2[h].at[me],
             send_sem=s2_sem.at[h],
-            recv_sem=r2_sem.at[h, me],
+            recv_sem=r2_sem.at[h, i // 2],
             device_id={"tm": d},
             device_id_type=MESH,
         )
@@ -335,14 +337,14 @@
         def _(i):
             both = apart(i)
             for s in range(2):
-                send(both[0], s)
+                send(i, both[0], s)
 
             @pl.when(i < RECORDS // 2 - 1)
             def _():
                 for s in range(2):
-                    send(both[1], s)
-
-        send(pair, 1 - side)
+                    send(i, both[1], s)
+
+        send(RECORDS // 2 - 1, pair, 1 - side)
 
     def await_all(ref, sem):
         pltpu.make_async_copy(ref, ref, sem).wait()
@@ -385,7 +387,10 @@
     message1(0, pair, 1 - side).start()
     for h in range(2):
         pltpu.make_async_copy(send1[h].at[pair, side], recv1[h].at[me], r1_sem.at[h]).start()
-    all_apart(lambda r, s: message1(1, r, s).start())
+    all_apart(lambda i, r, s: message1(1, r, s).start())
+
+    for copy in held[3:] + [load_target]:
+        copy.wait()
 
     for i in range(8):
         ttall[pl.ds(i * 128, 128), 0:OWN] = tbuf[:, i * 128 : (i + 1) * 128].T
@@ -460,8 +465,8 @@
                 send2[h][p, at, :] = g
 
     def back(h):
-        all_apart(lambda r, s: message2(h, 2 * r + s).start())
-        pltpu.make_async_copy(send2[h].at[me], recv2[h].at[me], r2_sem.at[h, me]).start()
+        all_apart(lambda i, r, s: message2(h, i, 2 * r + s).start())
+        pltpu.make_async_copy(send2[h].at[me], recv2[h].at[me], r2_sem.at[h, 3]).start()
 
     await_all(recv1a, r1_sem.at[0])
     over_devices(0)
@@ -494,11 +499,9 @@
         device_id_type=MESH,
     )
 
-    def await_back(both):
-        for r in both:
-            for d in (2 * r, 2 * r + 1):
-                for h in range(2):
-                    pltpu.make_async_copy(recv2[h].at[d], recv2[h].at[d], r2_sem.at[h, d]).wait()
+    def await_back(quarter):
+        for h in range(2):
+            await_all(recv2[h].at[pl.ds(0, DEVICES // 4)], r2_sem.at[h, quarter])
 
     def grad_power(both):
         powers = []
@@ -552,14 +555,13 @@
     @pl.loop(0, 2)
     def _(i):
         now = group(2 * i, 2)
-        for both in now:
-            await_back(both)
+        await_back(i)
         for both in now:
             back_to_wave(both, grad_power(both), True)
 
     final = group(4, 4)
-    for both in final:
-        await_back(both)
+    for quarter in (2, 3):
+        await_back(quarter)
     grads = [grad_power(both) for both in final]
     for both, grad in zip(final, grads):
         plus, minus = to_frames(both, grad, LOCAL - 8)
@@ -639,7 +641,7 @@
         pltpu.SemaphoreType.DMA((2,)),
         pltpu.SemaphoreType.DMA((2,)),
         pltpu.SemaphoreType.DMA((2,)),
-        pltpu.SemaphoreType.DMA((2, DEVICES)),
+        pltpu.SemaphoreType.DMA((2, 4)),
         pltpu.SemaphoreType.DMA((2,)),
     ]
     grad, losses = pl.pallas_call(

time: 58.5 us -> 58 us (level)
  no operation moved by 1% of the time
where the time goes in v8:
time: 58 us; the launch traced here: 57.9 us
  Pallas kernels  57.3 us (99%)
  between operations  0.64 us (1%)
    pallas_call x1, Pallas kernels, body(): pl.pallas_call(kernel, out_shape=(pltpu.VMEM((2, rows, 128), F32), jax.Sh...  55.9 us
    pallas_call x1, Pallas kernels, body(): pl.pallas_call(hand_over, out_shape=(jax.ShapeDtypeStruct((2, rows, 128),...  1.4 us

profile of v8, /device:TPU:56, one launch (start us, length us, event | category | flops | bytes accessed | tf_op | source)
XLA Modules:
  0.0 57.9 jit_solution(6559437314645945090)
XLA Ops:
  0.6 55.9 %shard_map.122 = (f32[2,2048,128]{2,1,0:T(8,128)S(1)}, f32[1,128]{1,0:T(1,128)}) custom-call(f32[2,2048,128]{2,1,0:T(8,128)} %bitcast.10, f32[48,1024]{1,0:T(8,128)} %target.1, s32[16]{0:T(128)} %lengths.1, bf16[768,512]{1,0:T(8,128)(2,1)} %constant.16.clone.h_forward, bf16[96,768]{1,0:T(8,128)(2,1)} %constant.17.clone.h_bands, ...), custom_call_target="tpu_custom_call" | custom-call | tf_op jit(solution)/shard_map/pallas_call | solution.py:647
  56.5 1.4 %shard_map.123 = (f32[2,2048,128]{2,1,0:T(8,128)}, f32[16]{0:T(128)}) custom-call(f32[2,2048,128]{2,1,0:T(8,128)S(1)} %get-tuple-element.6.grad, f32[1,128]{1,0:T(1,128)} %get-tuple-element.7.losses), custom_call_target="tpu_custom_call" | custom-call | tf_op jit(solution)/shard_map/pallas_call | solution.py:660

commit v9 on v8

--- a/solution.py
+++ b/solution.py
@@ -548,8 +548,15 @@
 
     def group(first, count):
         return [
-            [(pair + RECORDS // 2 - n) % RECORDS, (pair + RECORDS // 2 + 1 + n) % RECORDS]
-            for n in (first + m for m in range(count))
+            [
+                r
+                for n in (first + m, first + m + 1)
+                for r in (
+                    (pair + RECORDS // 2 - n) % RECORDS,
+                    (pair + RECORDS // 2 + 1 + n) % RECORDS,
+                )
+            ]
+            for m in range(0, count, 2)
         ]
 
     @pl.loop(0, 2)

time: 58 us -> 57.9 us (level)
  no operation moved by 1% of the time
where the time goes in v9:
time: 57.9 us; the launch traced here: 57.8 us
  Pallas kernels  57.1 us (99%)
  between operations  0.64 us (1%)
    pallas_call x1, Pallas kernels, body(): pl.pallas_call(kernel, out_shape=(pltpu.VMEM((2, rows, 128), F32), jax.Sh...  55.7 us
    pallas_call x1, Pallas kernels, body(): pl.pallas_call(hand_over, out_shape=(jax.ShapeDtypeStruct((2, rows, 128),...  1.4 us

profile of v9, /device:TPU:56, one launch (start us, length us, event | category | flops | bytes accessed | tf_op | source)
XLA Modules:
  0.0 57.8 jit_solution(6237678042275506983)
XLA Ops:
  0.6 55.7 %shard_map.122 = (f32[2,2048,128]{2,1,0:T(8,128)S(1)}, f32[1,128]{1,0:T(1,128)}) custom-call(f32[2,2048,128]{2,1,0:T(8,128)} %bitcast.10, f32[48,1024]{1,0:T(8,128)} %target.1, s32[16]{0:T(128)} %lengths.1, bf16[768,512]{1,0:T(8,128)(2,1)} %constant.16.clone.h_forward, bf16[96,768]{1,0:T(8,128)(2,1)} %constant.17.clone.h_bands, ...), custom_call_target="tpu_custom_call" | custom-call | tf_op jit(solution)/shard_map/pallas_call | solution.py:654
  56.4 1.4 %shard_map.123 = (f32[2,2048,128]{2,1,0:T(8,128)}, f32[16]{0:T(128)}) custom-call(f32[2,2048,128]{2,1,0:T(8,128)S(1)} %get-tuple-element.6.grad, f32[1,128]{1,0:T(1,128)} %get-tuple-element.7.losses), custom_call_target="tpu_custom_call" | custom-call | tf_op jit(solution)/shard_map/pallas_call | solution.py:667

commit v10 on v9

--- a/solution.py
+++ b/solution.py
@@ -566,7 +566,7 @@
         for both in now:
             back_to_wave(both, grad_power(both), True)
 
-    final = group(4, 4)
+    final = [sum(group(4, 4), [])]
     for quarter in (2, 3):
         await_back(quarter)
     grads = [grad_power(both) for both in final]

time: 57.9 us -> 58 us (level)
  no operation moved by 1% of the time
where the time goes in v10:
time: 58 us; the launch traced here: 57.9 us
  Pallas kernels  57.2 us (99%)
  between operations  0.64 us (1%)
    pallas_call x1, Pallas kernels, body(): pl.pallas_call(kernel, out_shape=(pltpu.VMEM((2, rows, 128), F32), jax.Sh...  55.8 us
    pallas_call x1, Pallas kernels, body(): pl.pallas_call(hand_over, out_shape=(jax.ShapeDtypeStruct((2, rows, 128),...  1.4 us

profile of v10, /device:TPU:56, one launch (start us, length us, event | category | flops | bytes accessed | tf_op | source)
XLA Modules:
  0.0 57.9 jit_solution(4253501468575978641)
XLA Ops:
  0.6 55.8 %shard_map.122 = (f32[2,2048,128]{2,1,0:T(8,128)S(1)}, f32[1,128]{1,0:T(1,128)}) custom-call(f32[2,2048,128]{2,1,0:T(8,128)} %bitcast.10, f32[48,1024]{1,0:T(8,128)} %target.1, s32[16]{0:T(128)} %lengths.1, bf16[768,512]{1,0:T(8,128)(2,1)} %constant.16.clone.h_forward, bf16[96,768]{1,0:T(8,128)(2,1)} %constant.17.clone.h_bands, ...), custom_call_target="tpu_custom_call" | custom-call | tf_op jit(solution)/shard_map/pallas_call | solution.py:654
  56.5 1.4 %shard_map.123 = (f32[2,2048,128]{2,1,0:T(8,128)}, f32[16]{0:T(128)}) custom-call(f32[2,2048,128]{2,1,0:T(8,128)S(1)} %get-tuple-element.6.grad, f32[1,128]{1,0:T(1,128)} %get-tuple-element.7.losses), custom_call_target="tpu_custom_call" | custom-call | tf_op jit(solution)/shard_map/pallas_call | solution.py:667
